TPU v7x, 512 devices: a whole 4x8x8 slice. The times are simulated.
512 devices in a mesh: seq: 64 (over z, x, core), tp: 8 (over y).
Axes of the slice: x: 4, y: 8, z: 8, core: 2. Of those that a mesh axis runs over, the one named last changes fastest.
Arguments:
- queries: bfloat16 [12288, 5120], P('seq', 'tp'), may hold values from -36 to 36
- keys: bfloat16 [12288, 1024], P('seq', 'tp'), may hold values from -4.5 to 4.5
- values: bfloat16 [12288, 1024], P('seq', 'tp'), may hold values from -6 to 6
- doc_ids: int32 [12288], P('seq'), may hold values from 0 to 5, never falling along the last dimension, each value on 1 to 6144 neighbouring positions
- w_out: bfloat16 [5120, 5120], P('tp', 'seq'), may hold values from -0.078125 to 0.078125
Outputs:
- mixed: bfloat16 [12288, 5120], P('seq', 'tp')
Inputs may be any that keep to these rules, and one draw needn't show every extreme that they name: `doc_ids`: document numbers never fall along the prompt; every one of them occurs, on 1 to 6144 consecutive positions, and one document is exactly 6144 long.
All inputs are finite; a program needn't handle non-finite values.
Results may differ from a plain program's by a relative error of at most 0.019.
Values may be sent and summed in bfloat16 or wider, within the bound.
A program may use at most 64 MiB of HBM per device.

v0:
```python
import math

import jax
import jax.numpy as jnp
from jax import lax
from jax.sharding import PartitionSpec as P

HEAD_WIDTH = 128


def attend_block(state, query_set, key_row_block, value_rows, key_docs, key_start):
    query_block, query_pos, query_doc = query_set
    top, total, summed = state
    token_rows = key_row_block.shape[0]
    local_heads = top.shape[0]
    head_size = key_row_block.shape[2]
    count_q = query_block.shape[0]
    key_pos = key_start + jnp.arange(token_rows, dtype=jnp.int32)
    visible = (key_docs[None, :] == query_doc[:, None]) & (key_pos[None, :] <= query_pos[:, None])

    def compute(carried):
        old_top, old_total, old_summed = carried
        scores = jnp.einsum(
            "ikgd,jkd->kgij", query_block, key_row_block, preferred_element_type=jnp.float32
        )
        scores = scores.reshape(local_heads, count_q, token_rows) / math.sqrt(head_size)
        masked = jnp.where(visible[None], scores, -1e30)
        new_top = jnp.maximum(old_top, jnp.max(masked, axis=2))
        keep = jnp.exp(old_top - new_top)
        weights = jnp.where(visible[None], jnp.exp(masked - new_top[:, :, None]), 0.0)
        new_total = old_total * keep + jnp.sum(weights, axis=2)
        grouped = weights.reshape(key_row_block.shape[1], -1, count_q, token_rows)
        product = jnp.einsum(
            "kgij,jkd->kgid",
            grouped,
            value_rows.astype(jnp.float32),
            precision=lax.Precision.HIGHEST,
        )
        new_summed = old_summed * keep[:, :, None] + product.reshape(
            local_heads, count_q, head_size
        )
        return (new_top, new_total, new_summed)

    return lax.cond(jnp.any(visible), compute, lambda carried: carried, state)


def attend_sets(query_sets, keys, values, doc_ids, local_heads, head_size):
    kv_heads = keys.shape[1] // head_size
    initial = tuple(
        (
            (
                jnp.full((local_heads, qs[0].shape[0]), -1e30, jnp.float32),
                jnp.zeros((local_heads, qs[0].shape[0]), jnp.float32),
                jnp.zeros((local_heads, qs[0].shape[0], head_size), jnp.float32),
            )
            for qs in query_sets
        )
    )
    key_piece = lax.all_gather(keys, "seq", axis=0, tiled=True)
    value_piece = lax.all_gather(values, "seq", axis=0, tiled=True)
    doc_piece = lax.all_gather(doc_ids, "seq", axis=0, tiled=True)
    token_rows = key_piece.shape[0]
    sub = math.gcd(token_rows, 512)

    def one_sub(index, states):
        offset = index * sub
        key_row_block = lax.dynamic_slice_in_dim(key_piece, offset, sub, 0).reshape(
            sub, kv_heads, head_size
        )
        value_rows = lax.dynamic_slice_in_dim(value_piece, offset, sub, 0).reshape(
            sub, kv_heads, head_size
        )
        key_docs = lax.dynamic_slice_in_dim(doc_piece, offset, sub, 0)
        return tuple(
            (
                attend_block(state, query_set, key_row_block, value_rows, key_docs, offset)
                for state, query_set in zip(states, query_sets)
            )
        )

    finals = lax.fori_loop(0, token_rows // sub, one_sub, initial)
    results = []
    for top, total, summed in finals:
        attended = summed / total[:, :, None]
        results.append(
            attended.transpose(1, 0, 2)
            .reshape(attended.shape[1], local_heads * head_size)
            .astype(jnp.bfloat16)
        )
    return results


def local(queries, keys, values, doc_ids, w_out):
    rows_dev = queries.shape[0]
    head_size = HEAD_WIDTH
    local_heads = queries.shape[1] // head_size
    kv_heads = keys.shape[1] // head_size
    group_width = local_heads // kv_heads
    own = lax.axis_index("seq")
    own_pos = own * rows_dev + jnp.arange(rows_dev, dtype=jnp.int32)
    shaped = queries.reshape(rows_dev, kv_heads, group_width, head_size)
    whole_set = (shaped, own_pos, doc_ids)
    attended = attend_sets((whole_set,), keys, values, doc_ids, local_heads, head_size)[0]
    partial_sums = jnp.dot(
        attended,
        lax.all_gather(w_out, "seq", axis=1, tiled=True),
        preferred_element_type=jnp.float32,
    )
    return lax.psum_scatter(
        partial_sums.astype(jnp.bfloat16), "tp", scatter_dimension=1, tiled=True
    )


def solution(mesh):
    placed = (P("seq", "tp"), P("seq", "tp"), P("seq", "tp"), P("seq"), P("tp", "seq"))
    return jax.shard_map(
        local, mesh=mesh, in_specs=placed, out_specs=P("seq", "tp"), check_vma=False
    )
```

profile of v0, /device:TPU:6, one launch (start us, length us, event | category | flops | bytes accessed | tf_op | source)
XLA Modules:
  0.0 420.2 jit_solution(13807645816460010386)
XLA Ops:
  6.5 0.7 all-gather.4.cloned.1.call-update
  7.3 0.7 all-gather.6.cloned.1.call-update
  8.1 0.7 all-gather.8.cloned.1.call-update
  8.8 1.1 copy.9
  10.1 1.3 dynamic-slice
  12.1 0.9 dynamic-update-slice
  13.0 242.5 %all-reduce = s32[12288]{0:T(1024)S(1)} all-reduce(s32[12288]{0:T(1024)S(1)} %dynamic-update-slice), channel_id=1, replica_groups=mesh['seq'=64,'tp'=8] {'seq'}, use_global_device_ids=true, to_apply=%add | all-reduce | flops 12288 | bytes 98304
  255.5 52.8 %while.18 = (s32[]{:T(128)}, f32[5,192]{1,0:T(8,128)S(1)}, f32[5,192]{1,0:T(8,128)S(1)}, f32[5,192,128]{2,1,0:T(8,128)S(1)}, s32[12288]{0:T(1024)S(1)}, /*index=...) while((s32[]{:T(128)}, f32[5,192]{1,0:T(8,128)S(1)}, ...), condition=%wide.region_6.7_spmd.clone, body=%wide.region_0.6_spmd.clone.sunk | while | flops 887343680 | bytes 7857733 | solution.py:81
  255.7 0.8 fusion.34
  257.1 4.9 %conditional.3 = ((f32[5,192]{1,0:T(8,128)S(1)}, f32[5,192]{1,0:T(8,128)S(1)}, f32[5,192,128]{2,1,0:T(8,128)S(1)})) conditional(s32[]{:T(128)} %convert_element_type.30, (f32[5,192]{1,0:T(8,128)S(1)}, f32[5,192]{1,0:T(8,128)S(1)}, f32[5,192,128]{2,1,0:T(8,128)S(1)}) %tuple.53, (pred[192,512]{1,0:T(8,128)(4,1)S(1)}, bf16[12288,128]{1,0:T(8,128)(2,1)}, ...), branch_computations={%region_2.0_spmd, %region_3.5_spmd} | conditional | flops 886949760 | bytes 7746592 | solution.py:44
  257.1 1.5 fusion.8
  258.6 0.7 select_reduce_fusion
  259.4 2.6 fusion.10
  262.2 0.8 fusion.34
  263.6 4.9 %conditional.3 = ((f32[5,192]{1,0:T(8,128)S(1)}, f32[5,192]{1,0:T(8,128)S(1)}, f32[5,192,128]{2,1,0:T(8,128)S(1)})) conditional(s32[]{:T(128)} %convert_element_type.30, (f32[5,192]{1,0:T(8,128)S(1)}, f32[5,192]{1,0:T(8,128)S(1)}, f32[5,192,128]{2,1,0:T(8,128)S(1)}) %tuple.53, (pred[192,512]{1,0:T(8,128)(4,1)S(1)}, bf16[12288,128]{1,0:T(8,128)(2,1)}, ...), branch_computations={%region_2.0_spmd, %region_3.5_spmd} | conditional | flops 886949760 | bytes 7746592 | solution.py:44
  263.6 1.5 fusion.8
  265.1 0.7 select_reduce_fusion
  265.9 2.6 fusion.10
  268.7 0.8 fusion.34
  270.1 4.9 %conditional.3 = ((f32[5,192]{1,0:T(8,128)S(1)}, f32[5,192]{1,0:T(8,128)S(1)}, f32[5,192,128]{2,1,0:T(8,128)S(1)})) conditional(s32[]{:T(128)} %convert_element_type.30, (f32[5,192]{1,0:T(8,128)S(1)}, f32[5,192]{1,0:T(8,128)S(1)}, f32[5,192,128]{2,1,0:T(8,128)S(1)}) %tuple.53, (pred[192,512]{1,0:T(8,128)(4,1)S(1)}, bf16[12288,128]{1,0:T(8,128)(2,1)}, ...), branch_computations={%region_2.0_spmd, %region_3.5_spmd} | conditional | flops 886949760 | bytes 7746592 | solution.py:44
  270.1 1.5 fusion.8
  271.6 0.7 select_reduce_fusion
  272.4 2.6 fusion.10
  275.2 0.8 fusion.34
  276.8 0.8 fusion.34
  278.3 0.8 fusion.34
  279.9 0.8 fusion.34
  281.5 0.8 fusion.34
  283.1 0.8 fusion.34
  284.7 0.8 fusion.34
  286.3 0.8 fusion.34
  287.9 0.8 fusion.34
  289.5 0.8 fusion.34
  291.0 0.8 fusion.34
  292.6 0.8 fusion.34
  294.2 0.8 fusion.34
  295.8 0.8 fusion.34
  297.4 0.8 fusion.34
  299.0 0.8 fusion.34
  300.6 0.8 fusion.34
  302.2 0.8 fusion.34
  303.7 0.8 fusion.34
  305.3 0.8 fusion.34
  306.9 0.8 fusion.34
  308.8 5.3 %convolution_convert_fusion = bf16[192,5120]{1,0:T(8,128)(2,1)S(1)} fusion(bf16[192,640]{0,1:T(8,128)(2,1)S(1)} %bitcast.52, bf16[640,5120]{0,1:T(8,128)(2,1)} %all-gather.8.cloned.1.call-done), kind=kOutput, calls=%fused_computation.33 | convolution fusion | flops 1259274240 | bytes 8765440 | tf_op jit(solution)/shard_map/dot_general | solution.py:104
  314.1 2.5 copy.12
  316.7 95.2 %reduce-scatter.4.cloned.1.call-done = bf16[640,192]{1,0:T(8,128)(2,1)} async-done(((bf16[5120,192]{1,0:T(8,128)(2,1)}), bf16[640,192]{1,0:T(8,128)(2,1)}) %reduce-scatter.4.cloned.1.call-update) | async-done | bytes 245776
  411.8 1.8 copy.13
  (119 shorter events, 3.2 us)
Async XLA Ops:
  6.5 249.0 %copy-start = (s32[192]{0:T(256)S(1)}, s32[192]{0:T(256)}, u32[]{:S(2)}) copy-start(s32[192]{0:T(256)} %param.12) | copy-start | bytes 2308
  6.5 249.0 %all-gather.4.cloned.1.call-start = ((), (), s32[]{:S(2)}) async-start(), calls=%async_computation.1 | async-start | bytes 3194880 | tf_op jit(solution)/shard_map/all_gather | solution.py:59
  7.3 248.2 %all-gather.6.cloned.1.call-start = ((), (), s32[]{:S(2)}) async-start(), calls=%async_computation.2 | async-start | bytes 3194880 | tf_op jit(solution)/shard_map/all_gather | solution.py:60
  8.0 300.8 %all-gather.8.cloned.1.call-start = ((), (), s32[]{:S(2)}) async-start(), calls=%async_computation.3 | async-start | bytes 6656000 | tf_op jit(solution)/shard_map/all_gather | solution.py:106
  8.7 403.1 %reduce-scatter.4.cloned.1.call-start = ((), (), s32[]{:S(2)}) async-start(), calls=%async_computation.4 | async-start | bytes 2949120
Sparse Core Ops, SparseCore 0:
  10.7 87.8 all-gather.3
  102.0 81.4 all-gather.5
  186.7 84.1 all-gather.7
  316.8 95.0 reduce-scatter.3
where the time goes:
time: 421 us; the launch traced here: 420 us
  blocking collectives  243 us (58%)
  waiting for transfers between devices  97.3 us (23%)
  other arithmetic  22.5 us (5%)
  matrix products  17.7 us (4%)
  loops' own time  16.3 us (4%)
  between operations  13.8 us (3%)
  local copies, waits for them, and re-layouts  9.97 us (2%)
    unnamed x1, blocking collectives  243 us
    unnamed x5, waiting for transfers between devices  97.3 us
    reduce_or x24, other arithmetic, attend_block(): return lax.cond(jnp.any(visible), compute, lambda carried: carried, state)  19.7 us
    another operation x1, loops' own time, attend_sets(): finals = lax.fori_loop(0, token_rows // sub, one_sub, initial)  15.9 us
  transfers between devices with their start and end apart: 4, of which 1 were waited for; matrix products, arithmetic and copies ran while one was open for 10% of the time, Pallas kernels for 0%

commit v1 on v0

v1 whole, which is shorter than its diff:
```python
import functools
import math

import jax
import jax.numpy as jnp
from jax import lax
from jax.experimental import pallas as pl
from jax.experimental.pallas import tpu as pltpu
from jax.sharding import PartitionSpec as P

MESH = pl.DeviceIdType.MESH
F32, BF16 = jnp.float32, jnp.bfloat16
NT = (((1,), (1,)), ((), ()))

NZ, NX, NY = 8, 4, 8
T = 192
HEADS = 5
W = 128
STAT = 16
KVR = T + STAT
DEPTH = 5
COLS = 80
K = HEADS * W
GROUP = 48
PACK = T + GROUP
SCALE = math.log2(math.e) / math.sqrt(W)
HIDE = -131072.0


def dot_nt(a, b):
    return lax.dot_general(a, b, NT, preferred_element_type=F32)


def split_of(j):
    return 128 if j < 2 else 112


def kernel(q_ref, k_ref, v_ref, d_ref, w_ref, o_ref,
           kv, ff, qa, acc, top, wz, wr, ag, sbuf, rbuf, fsend, fin, selm, selr,
           kvz_s, kvz_r, kvx_s, kvx_r, kvd_s, kvd_r, wz_s, wz_r, wd_s, wd_r,
           ax_s, ax_r, rs_s, rs_r, fx_s, fx_r):
    s = lax.axis_index("seq")
    t = lax.axis_index("tp")
    z, x, c = s // 8, lax.rem(s // 2, 4), lax.rem(s, 2)
    me = x * 2 + c

    def dev(dz=0, dx=0, dc=0, dy=0):
        zz = lax.rem(z + dz + NZ, NZ)
        xx = lax.rem(x + dx + NX, NX)
        cc = lax.rem(c + dc, 2)
        return (zz * 8 + xx * 2 + cc, lax.rem(t + dy + NY, NY))

    up, down = dev(dz=1), dev(dz=-1)
    right, left = dev(dx=1), dev(dx=-1)
    sib = dev(dc=1)
    xr, xl, xo = lax.rem(x + 1, NX), lax.rem(x + 3, NX), lax.rem(x + 2, NX)
    oc = 1 - c

    def rc(ref, ss, rs, to):
        return pltpu.make_async_remote_copy(
            src_ref=ref, dst_ref=ref, send_sem=ss, recv_sem=rs, device_id=to, device_id_type=MESH)

    barrier = pltpu.get_barrier_semaphore()
    peers = [up, down, right, left, dev(dx=2), sib, dev(dy=1), dev(dy=-1)]
    for peer in peers:
        pl.semaphore_signal(barrier, inc=1, device_id=peer, device_id_type=MESH)

    kv[0, c, x, 0:T, 0:W] = k_ref[...]
    kv[0, c, x, 0:T, W:2 * W] = v_ref[...]
    docs = jnp.broadcast_to(d_ref[...], (W, T))
    number = lax.broadcasted_iota(jnp.int32, (W, T), 0)
    first = jnp.sum((docs < number).astype(F32), axis=1, keepdims=True)
    last = jnp.sum((docs <= number).astype(F32), axis=1, keepdims=True)
    first = jnp.transpose(jnp.broadcast_to(first, (W, W)))
    last = jnp.transpose(jnp.broadcast_to(last, (W, W)))
    stat = jnp.concatenate([first[0:8], last[0:8]], axis=0).astype(BF16)
    kv[0, c, x, T:KVR, 0:W] = stat
    kv[0, c, x, T:KVR, W:2 * W] = jnp.zeros((STAT, W), BF16)
    wz[z, c] = w_ref[...]

    pl.semaphore_wait(barrier, len(peers))

    started = []

    def go(copy):
        copy.start()
        started.append(copy)

    def x_start(p):
        blk = kv.at[p, c, x]
        go(rc(blk, kvx_s.at[p, 0], kvx_r.at[p, 0], right))
        go(rc(blk, kvx_s.at[p, 1], kvx_r.at[p, 1], left))
        go(rc(blk, kvd_s.at[p, 0], kvd_r.at[p, 0], sib))

    def x_relay(p):
        rc(kv.at[p, c, xl], kvx_s.at[p, 0], kvx_r.at[p, 0], right).wait_recv()
        go(rc(kv.at[p, c, xl, pl.ds(0, 96)], kvx_s.at[p, 2], kvx_r.at[p, 2], right))
        go(rc(kv.at[p, c, xl], kvd_s.at[p, 1], kvd_r.at[p, 1], sib))
        rc(kv.at[p, c, xr], kvx_s.at[p, 1], kvx_r.at[p, 1], left).wait_recv()
        go(rc(kv.at[p, c, xr, pl.ds(96, 112)], kvx_s.at[p, 3], kvx_r.at[p, 3], left))
        go(rc(kv.at[p, c, xr], kvd_s.at[p, 2], kvd_r.at[p, 2], sib))

    def x_end(p):
        rc(kv.at[p, c, xo, pl.ds(0, 96)], kvx_s.at[p, 2], kvx_r.at[p, 2], right).wait_recv()
        rc(kv.at[p, c, xo, pl.ds(96, 112)], kvx_s.at[p, 3], kvx_r.at[p, 3], left).wait_recv()
        go(rc(kv.at[p, c, xo], kvd_s.at[p, 3], kvd_r.at[p, 3], sib))

    def sib_wait(p):
        for i, xx in enumerate((x, xl, xr, xo)):
            rc(kv.at[p, oc, xx], kvd_s.at[p, i], kvd_r.at[p, i], sib).wait_recv()

    def z_send(p):
        return pltpu.make_async_remote_copy(
            src_ref=kv.at[p, c, x], dst_ref=kv.at[p + 1, c, x], send_sem=kvz_s.at[p], recv_sem=kvz_r.at[p],
            device_id=up, device_id_type=MESH)

    def z_step(p):
        z_send(p - 1).wait_recv()
        if p < DEPTH - 1:
            go(z_send(p))
        x_start(p)

    def w_down(i):
        return rc(wz.at[lax.rem(z + i, NZ), c], wz_s.at[i], wz_r.at[i], down)

    def w_up(i):
        return rc(wz.at[lax.rem(z - i + NZ, NZ), c], wz_s.at[4 + i], wz_r.at[4 + i], up)

    def w_sib(plane, i):
        return rc(wz.at[plane, c], wd_s.at[i], wd_r.at[i], sib)

    def w_down_step(i):
        plane = lax.rem(z + i, NZ)
        rc(wz.at[plane, c], wz_s.at[i - 1], wz_r.at[i - 1], down).wait_recv()
        if i < 4:
            go(w_down(i))
        go(w_sib(plane, i))

    def w_up_step(i):
        plane = lax.rem(z - i + NZ, NZ)
        rc(wz.at[plane, c], wz_s.at[3 + i], wz_r.at[3 + i], up).wait_recv()
        if i < 3:
            go(w_up(i))
        go(w_sib(plane, 4 + i))

    go(z_send(0))
    x_start(0)
    go(w_down(0))
    go(w_sib(z, 0))

    row = lax.broadcasted_iota(jnp.int32, (T, W), 0).astype(F32)

    def doc_rows(bounds):
        bounds = bounds.astype(F32)
        return jnp.where((row >= bounds[0:1]) & (row < bounds[8:9]), 1.0, 0.0)

    own_docs = doc_rows(stat)
    feature = jnp.where(own_docs > 0.5, 0.0, HIDE).astype(BF16)
    for h in range(HEADS):
        qa[h * T:(h + 1) * T, 0:W] = q_ref[:, h * W:(h + 1) * W]
        qa[h * T:(h + 1) * T, W:2 * W] = feature
    k_own = jnp.concatenate([k_ref[...], own_docs.astype(BF16)], axis=1)
    v_own = jnp.concatenate([v_ref[...], jnp.ones((T, W), BF16)], axis=1)
    causal = lax.broadcasted_iota(jnp.int32, (T, T), 0) >= lax.broadcasted_iota(jnp.int32, (T, T), 1)
    for h in range(HEADS):
        rows = slice(h * T, (h + 1) * T)
        scores = jnp.where(causal, dot_nt(qa[rows, :], k_own), -1e30)
        high = jnp.broadcast_to(jnp.max(scores, axis=1, keepdims=True) * SCALE, (T, W))
        weights = jnp.exp2(scores * SCALE - high[:, 0:1]).astype(BF16)
        top[rows, :] = high
        acc[rows, :] = jnp.dot(weights, v_own, preferred_element_type=F32)

    r5 = lax.broadcasted_iota(jnp.int32, (NX * W, K), 0)
    col = lax.broadcasted_iota(jnp.int32, (NX * W, K), 1)
    part, lane = r5 // W, lax.rem(r5, W)
    selm[...] = jnp.where(col == part * 160 + lane + jnp.where(lane < 64, 0, 16), 1.0, 0.0).astype(BF16)
    spot = lax.rem(lane, 32)
    goal = part * 160 + spot + jnp.where(spot < 16, 64, 128)
    for g in range(4):
        selr[g] = jnp.where((col == goal) & (lane // 32 == g), 1.0, 0.0).astype(BF16)
    wr[...] = jnp.zeros_like(wr)

    def attend(blocks, valid):
        for b in range(8):
            docs_b = doc_rows(kv[blocks[b], b // 4, b % 4, T:KVR, 0:W])
            ff[b] = jnp.where(valid[b], docs_b, 1.0).astype(BF16)
        half = HEADS * T // 2
        for u in range(2):
            rows = slice(u * half, (u + 1) * half)
            keys = jnp.concatenate([kv[blocks[b], b // 4, b % 4, 0:T, 0:W] for b in range(8)], axis=0)
            keys = jnp.concatenate([keys, ff[...].reshape(8 * T, W)], axis=1)
            scores = dot_nt(qa[rows, :], keys)
            old = top[rows, :]
            new = jnp.maximum(old, jnp.max(scores, axis=1, keepdims=True) * SCALE)
            weights = jnp.exp2(scores * SCALE - new[:, 0:1]).astype(BF16)
            vals = jnp.concatenate([kv[blocks[b], b // 4, b % 4, 0:T, W:2 * W] for b in range(8)], axis=0)
            vals = jnp.concatenate([vals, jnp.ones((8 * T, W), BF16)], axis=1)
            keep = jnp.exp2(old - new)
            acc[rows, :] = acc[rows, :] * jnp.concatenate([keep, keep], axis=1) + jnp.dot(
                weights, vals, preferred_element_type=F32)
            top[rows, :] = new

    def attend_plane(p):
        sib_wait(p)
        attend([p] * 8, [z >= p] * 8)

    z_step(1)
    x_relay(0)
    w_down_step(1)
    z_step(2)
    x_end(0)
    x_relay(1)
    z_step(3)
    x_end(1)
    attend_plane(1)
    z_step(4)
    go(w_up(0))
    x_relay(2)
    x_end(2)
    w_down_step(2)
    attend_plane(2)
    x_relay(3)
    w_down_step(3)
    w_up_step(1)
    x_end(3)
    attend_plane(3)
    x_relay(4)
    x_end(4)
    w_up_step(2)
    w_down_step(4)
    sib_wait(0)
    sib_wait(4)
    early = [(b % 4) * 2 + b // 4 < me for b in range(8)]
    attend([jnp.where(e, 0, 4) for e in early], [e | (z >= 4) for e in early])
    w_up_step(3)

    for h in range(HEADS):
        rows = slice(h * T, (h + 1) * T)
        ag[x, :, h * W:(h + 1) * W] = (acc[rows, 0:W] / acc[rows, W:2 * W]).astype(BF16)
    go(rc(ag.at[x], ax_s.at[0], ax_r.at[0], right))
    go(rc(ag.at[x], ax_s.at[1], ax_r.at[1], left))

    for i in range(NZ):
        plane = lax.rem(z + i, NZ) if i <= 4 else lax.rem(z - (i - 4) + NZ, NZ)
        rc(wz.at[plane, oc], wd_s.at[i], wd_r.at[i], sib).wait_recv()
    for o in range(NY):
        wr[o, 96:112, :] = wz[o, 0, 64:80, :]
        wr[o, 112:128, :] = wz[o, 1, 64:80, :]

    def main_cols(o):
        return jnp.concatenate([wz[o, 0, 0:64, :], wz[o, 1, 0:64, :]], axis=0)

    def part_up(j, o):
        return dot_nt(ag[lax.rem(x + j, NX), 0:split_of(j), :], main_cols(o))

    def part_down(j, o):
        xx = lax.rem(x + j, NX)
        main = dot_nt(ag[xx, split_of(j):T, :], main_cols(o))
        rest = dot_nt(ag[xx, 0:GROUP, :], wr[o, 96:224, :])
        for g in range(1, 4):
            rest += dot_nt(ag[xx, g * GROUP:(g + 1) * GROUP, :], wr[o, 96 - 32 * g:224 - 32 * g, :])
        return jnp.concatenate([main, rest], axis=0)

    y_up, y_down = dev(dy=1), dev(dy=-1)

    def rs(d, k, j):
        n = split_of(j) if d == 0 else PACK - split_of(j)
        return pltpu.make_async_remote_copy(
            src_ref=sbuf.at[d, k, j, pl.ds(0, n)], dst_ref=rbuf.at[d, k, j, pl.ds(0, n)],
            send_sem=rs_s.at[d, k, j], recv_sem=rs_r.at[d, k, j],
            device_id=y_up if d == 0 else y_down, device_id_type=MESH)

    def step(d, k, j, first_step):
        o = lax.rem(t + 7 - k, NY) if d == 0 else lax.rem(t + 1 + k, NY)
        n = split_of(j) if d == 0 else PACK - split_of(j)
        total = part_up(j, o) if d == 0 else part_down(j, o)
        if not first_step:
            rs(d, k - 1, j).wait_recv()
            total = total + rbuf[d, k - 1, j, 0:n, :].astype(F32)
        return total

    def send_step(k, first_step):
        for j in range(NX):
            if first_step and j == 1:
                rc(ag.at[xr], ax_s.at[1], ax_r.at[1], left).wait_recv()
                go(rc(ag.at[xr, pl.ds(96, 96)], ax_s.at[3], ax_r.at[3], left))
                rc(ag.at[xl], ax_s.at[0], ax_r.at[0], right).wait_recv()
                go(rc(ag.at[xl, pl.ds(0, 96)], ax_s.at[2], ax_r.at[2], right))
            if first_step and j == 2:
                rc(ag.at[xo, pl.ds(0, 96)], ax_s.at[2], ax_r.at[2], right).wait_recv()
                rc(ag.at[xo, pl.ds(96, 96)], ax_s.at[3], ax_r.at[3], left).wait_recv()
            for d in range(2):
                n = split_of(j) if d == 0 else PACK - split_of(j)
                sbuf[d, k, j, 0:n, :] = step(d, k, j, first_step).astype(BF16)
                rs(d, k, j).start()

    send_step(0, True)

    def loop(k, carry):
        send_step(k, False)
        return carry

    lax.fori_loop(1, 7, loop, 0)

    def fx(j):
        to = lax.rem(x + j, NX)
        return pltpu.make_async_remote_copy(
            src_ref=fsend.at[j - 1], dst_ref=fin.at[x], send_sem=fx_s.at[j - 1], recv_sem=fx_r.at[j - 1],
            device_id=(z * 8 + to * 2 + c, t), device_id_type=MESH)

    for j in (1, 2, 3, 0):
        block = jnp.concatenate([step(0, 7, j, False), step(1, 7, j, False)], axis=0).astype(BF16)
        if j == 0:
            fin[x] = block
        else:
            fsend[j - 1] = block
            go(fx(j))
    for j in (1, 2, 3):
        pltpu.make_async_remote_copy(
            src_ref=fsend.at[j - 1], dst_ref=fin.at[lax.rem(x - j + NX, NX)], send_sem=fx_s.at[j - 1],
            recv_sem=fx_r.at[j - 1], device_id=dev(dx=j), device_id_type=MESH).wait_recv()

    main = jnp.concatenate([fin[i, 0:T, :] for i in range(NX)], axis=1)
    rest = jnp.concatenate([fin[i, T:PACK, :] for i in range(NX)], axis=1)
    for g in range(4):
        rows = slice(g * GROUP, (g + 1) * GROUP)
        o_ref[rows, :] = (
            jnp.dot(main[rows, :], selm[...], preferred_element_type=F32)
            + jnp.dot(rest, selr[g], preferred_element_type=F32)).astype(BF16)

    for copy in started:
        copy.wait_send()

    def drain(k, carry):
        for j in range(NX):
            for d in range(2):
                rs(d, k, j).wait_send()
        return carry

    lax.fori_loop(0, 7, drain, 0)


def local(queries, keys, values, doc_ids, w_out):
    sem = pltpu.SemaphoreType.DMA
    vmem = pl.BlockSpec(memory_space=pltpu.VMEM)
    return pl.pallas_call(
        kernel,
        out_shape=jax.ShapeDtypeStruct((T, K), BF16),
        in_specs=[vmem] * 5,
        out_specs=vmem,
        scratch_shapes=[
            pltpu.VMEM((DEPTH, 2, NX, KVR, 2 * W), BF16),
            pltpu.VMEM((8, T, W), BF16),
            pltpu.VMEM((HEADS * T, 2 * W), BF16),
            pltpu.VMEM((HEADS * T, 2 * W), F32),
            pltpu.VMEM((HEADS * T, W), F32),
            pltpu.VMEM((NZ, 2, COLS, K), BF16),
            pltpu.VMEM((NY, 224, K), BF16),
            pltpu.VMEM((NX, T, K), BF16),
            pltpu.VMEM((2, 7, NX, 128, W), BF16),
            pltpu.VMEM((2, 7, NX, 128, W), BF16),
            pltpu.VMEM((3, PACK, W), BF16),
            pltpu.VMEM((NX, PACK, W), BF16),
            pltpu.VMEM((NX * W, K), BF16),
            pltpu.VMEM((4, NX * W, K), BF16),
            sem((4,)), sem((4,)), sem((5, 4)), sem((5, 4)), sem((5, 4)), sem((5, 4)),
            sem((7,)), sem((7,)), sem((8,)), sem((8,)),
            sem((4,)), sem((4,)), sem((2, 7, NX)), sem((2, 7, NX)), sem((3,)), sem((3,)),
        ],
        compiler_params=pltpu.CompilerParams(
            collective_id=0, has_side_effects=True, vmem_limit_bytes=56 * 2**20),
        name="attend_project",
    )(queries, keys, values, doc_ids.reshape(1, T), w_out.T)


def solution(mesh):
    placed = (P("seq", "tp"), P("seq", "tp"), P("seq", "tp"), P("seq"), P("tp", "seq"))
    return jax.shard_map(
        local, mesh=mesh, in_specs=placed, out_specs=P("seq", "tp"), check_vma=False
    )
```

time: 421 us -> 105 us (0.25)
  blocking collectives: 243 us -> 0 us
  Pallas kernels: 0 us -> 104 us
  waiting for transfers between devices: 97.3 us -> 0 us
  other arithmetic: 22.5 us -> 0 us
  matrix products: 17.7 us -> 0 us
  loops' own time: 16.3 us -> 0 us
  between operations: 13.8 us -> 0.01 us
  local copies, waits for them, and re-layouts: 9.97 us -> 1.66 us
    unnamed x1 -> x0, blocking collectives: 243 us -> none
    pallas_call x0 -> x1, Pallas kernels: none -> 104 us  [local(): pl.pallas_call(kernel, out_shape=jax.ShapeDtypeStruct((T, K), BF16), in_s...]
    unnamed x5 -> x0, waiting for transfers between devices: 97.3 us -> none
    reduce_or x24 -> x0, other arithmetic: 19.7 us -> none  [attend_block(): return lax.cond(jnp.any(visible), compute, lambda carried: carried, state)]
    dot_general x7 -> x0, matrix products: 17.7 us -> none  [the longest x3 7.95 us: compute(): jnp.einsum('kgij,jkd->kgid', grouped, value_rows.astype(jnp.float32), pre...]
    another operation x25 -> x0, loops' own time: 16.3 us -> none  [the longest x1 15.9 us: attend_sets(): finals = lax.fori_loop(0, token_rows // sub, one_sub, initial)]
    unnamed x9 -> x1, local copies, waits for them, and re-layouts: 7.88 us -> 1.66 us
  transfers between devices with their start and end apart: 4 -> 0, of which waited for: 1 -> 0; matrix products, arithmetic and copies ran while one was open for 10% -> 0% of each run, Pallas kernels for 0% -> 0%
where the time goes in v1:
time: 105 us
  Pallas kernels  104 us (99%)
  local copies, waits for them, and re-layouts  1.66 us (2%)
    pallas_call x1, Pallas kernels, local(): pl.pallas_call(kernel, out_shape=jax.ShapeDtypeStruct((T, K), BF16), in_s...  104 us

profile of v1, /device:TPU:6, one launch (start us, length us, event | category | flops | bytes accessed | tf_op | source)
XLA Modules:
  0.0 105.2 jit_solution(3741478308799295451)
XLA Ops:
  0.0 103.5 %attend_project.1 = bf16[192,640]{1,0:T(8,128)(2,1)} custom-call(bf16[192,640]{1,0:T(8,128)(2,1)} %q_ref.1, bf16[192,128]{1,0:T(8,128)(2,1)} %k_ref.1, bf16[192,128]{1,0:T(8,128)(2,1)} %v_ref.1, s32[1,192]{1,0:T(1,128)} %bitcast.3, bf16[80,640]{1,0:T(8,128)(2,1)} %bitcast.2), custom_call_target="tpu_custom_call" | custom-call | tf_op jit(solution)/shard_map/attend_project/pallas_call | solution.py:346
  103.5 1.7 %copy.7 = bf16[192,640]{1,0:T(8,128)(2,1)} copy(bf16[192,640]{1,0:T(8,128)(2,1)} %attend_project.1) | data formatting | bytes 491520

commit v2 on v1

v2 whole, which is shorter than its diff:
```python
import functools
import math

import jax
import jax.numpy as jnp
from jax import lax
from jax.experimental import pallas as pl
from jax.experimental.pallas import tpu as pltpu
from jax.sharding import PartitionSpec as P

MESH = pl.DeviceIdType.MESH
F32, BF16 = jnp.float32, jnp.bfloat16
NT = (((1,), (1,)), ((), ()))

NZ, NX, NY = 8, 4, 8
T = 192
HEADS = 5
W = 128
STAT = 16
KVR = T + STAT
DEPTH = 5
COLS = 80
K = HEADS * W
GROUP = 48
PACK = T + GROUP
SCALE = math.log2(math.e) / math.sqrt(W)
HIDE = -131072.0


def dot_nt(a, b):
    return lax.dot_general(a, b, NT, preferred_element_type=F32)


def kernel(q_hbm, k_hbm, v_hbm, d_hbm, w_hbm, o_ref,
           kv, ff, qv, dv, qa, acc, top, wz, wr, ag, sbuf, rbuf, fsend, fin, selm, selr,
           in_s, kvz_s, kvz_r, kvx_s, kvx_r, kvd_s, kvd_r, wz_s, wz_r, wd_s, wd_r,
           ax_s, ax_r, rs_s, rs_r, fx_s, fx_r):
    s = lax.axis_index("seq")
    t = lax.axis_index("tp")
    z, x, c = s // 8, lax.rem(s // 2, 4), lax.rem(s, 2)
    me = x * 2 + c

    def dev(dz=0, dx=0, dc=0, dy=0):
        zz = lax.rem(z + dz + NZ, NZ)
        xx = lax.rem(x + dx + NX, NX)
        cc = lax.rem(c + dc, 2)
        return (zz * 8 + xx * 2 + cc, lax.rem(t + dy + NY, NY))

    up, right, left, across = dev(dz=1), dev(dx=1), dev(dx=-1), dev(dx=2)
    sib = dev(dc=1)
    xr, xl, xo = lax.rem(x + 1, NX), lax.rem(x + 3, NX), lax.rem(x + 2, NX)
    oc = 1 - c

    def rc(ref, ss, rs, to):
        return pltpu.make_async_remote_copy(
            src_ref=ref, dst_ref=ref, send_sem=ss, recv_sem=rs, device_id=to, device_id_type=MESH)

    barrier = pltpu.get_barrier_semaphore()
    peers = [dev(dz=i) for i in range(1, NZ)] + [right, left, across, sib, dev(dy=1), dev(dy=-1)]
    for peer in peers:
        pl.semaphore_signal(barrier, inc=1, device_id=peer, device_id_type=MESH)
    loads = [
        pltpu.make_async_copy(d_hbm, dv, in_s.at[0]),
        pltpu.make_async_copy(k_hbm, kv.at[0, c, x, pl.ds(0, T), pl.ds(0, W)], in_s.at[1]),
        pltpu.make_async_copy(v_hbm, kv.at[0, c, x, pl.ds(0, T), pl.ds(W, W)], in_s.at[2]),
        pltpu.make_async_copy(w_hbm, wz.at[z, c], in_s.at[3]),
        pltpu.make_async_copy(q_hbm, qv, in_s.at[4]),
    ]
    for load in loads:
        load.start()

    loads[0].wait()
    docs = jnp.broadcast_to(dv[...], (W, T))
    number = lax.broadcasted_iota(jnp.int32, (W, T), 0)
    first = jnp.sum((docs < number).astype(F32), axis=1, keepdims=True)
    last = jnp.sum((docs <= number).astype(F32), axis=1, keepdims=True)
    first = jnp.transpose(jnp.broadcast_to(first, (W, W)))
    last = jnp.transpose(jnp.broadcast_to(last, (W, W)))
    stat = jnp.concatenate([first[0:8], last[0:8]], axis=0).astype(BF16)
    kv[0, c, x, T:KVR, 0:W] = stat
    kv[0, c, x, T:KVR, W:2 * W] = jnp.zeros((STAT, W), BF16)
    loads[1].wait()
    loads[2].wait()

    pl.semaphore_wait(barrier, len(peers))

    started = []

    def go(copy):
        copy.start()
        started.append((copy, None))

    def go_if(cond, copy):
        @pl.when(cond)
        def _():
            copy.start()
        started.append((copy, cond))

    def z_copy(p, half):
        rows = pl.ds(0, 96) if half == 0 else pl.ds(96, KVR - 96)
        return pltpu.make_async_remote_copy(
            src_ref=kv.at[p, c, x, rows], dst_ref=kv.at[p + 1, c, x, rows], send_sem=kvz_s.at[p, half],
            recv_sem=kvz_r.at[p, half], device_id=up, device_id_type=MESH)

    def x_start(p):
        blk = kv.at[p, c, x]
        go(rc(blk, kvx_s.at[p, 0], kvx_r.at[p, 0], right))
        go(rc(blk, kvx_s.at[p, 1], kvx_r.at[p, 1], left))
        go(rc(blk, kvx_s.at[p, 2], kvx_r.at[p, 2], across))
        go(rc(blk, kvd_s.at[p, 0], kvd_r.at[p, 0], sib))

    def side(dest):
        return jnp.where(x < dest, 0, 4)

    def x_start_mixed(p):
        for i, (to, dest) in enumerate(((right, xr), (left, xl), (across, xo))):
            blk = kv.at[p, c, x]
            go_if((x < dest) if p == 0 else (x > dest), rc(blk, kvx_s.at[p, i], kvx_r.at[0, i], to))
        go_if(c == (0 if p == 0 else 1), rc(kv.at[p, c, x], kvd_s.at[p, 0], kvd_r.at[0, 0], sib))

    def plane_of(p, xx):
        return p if p > 0 else jnp.where(xx < x, 0, 4)

    def x_end(p):
        for i, xx in enumerate((xl, xr, xo)):
            ref = kv.at[plane_of(p, xx), c, xx]
            rc(ref, kvx_s.at[p, i], kvx_r.at[p, i], right).wait_recv()
            go(rc(ref, kvd_s.at[p, i + 1], kvd_r.at[p, i + 1], sib))

    def sib_wait(p):
        own = p if p > 0 else jnp.where(c == 1, 0, 4)
        for i, (pp, xx) in enumerate(((own, x), (plane_of(p, xl), xl), (plane_of(p, xr), xr), (plane_of(p, xo), xo))):
            rc(kv.at[pp, oc, xx], kvd_s.at[p, i], kvd_r.at[p, i], sib).wait_recv()

    def z_step(p):
        for half in range(2):
            z_copy(p - 1, half).wait_recv()
            if p < DEPTH - 1:
                go(z_copy(p, half))
        if p < DEPTH - 1:
            x_start(p)
        else:
            x_start_mixed(p)

    def w_send(i):
        go(rc(wz.at[z, c], wz_s.at[i], wz_r.at[i], dev(dz=-i)))

    def w_recv(i):
        ref = wz.at[lax.rem(z + i, NZ), c]
        rc(ref, wz_s.at[i], wz_r.at[i], up).wait_recv()
        go(rc(ref, wd_s.at[i], wd_r.at[i], sib))

    go(z_copy(0, 0))
    go(z_copy(0, 1))
    x_start_mixed(0)
    loads[3].wait()
    for i in (1, 2, 3, 4):
        w_send(i)
    go(rc(wz.at[z, c], wd_s.at[0], wd_r.at[0], sib))

    row = lax.broadcasted_iota(jnp.int32, (T, W), 0).astype(F32)

    def doc_rows(bounds):
        bounds = bounds.astype(F32)
        return jnp.where((row >= bounds[0:1]) & (row < bounds[8:9]), 1.0, 0.0)

    own_docs = doc_rows(stat)
    feature = jnp.where(own_docs > 0.5, 0.0, HIDE).astype(BF16)
    loads[4].wait()
    for h in range(HEADS):
        qa[h * T:(h + 1) * T, 0:W] = qv[:, h * W:(h + 1) * W]
        qa[h * T:(h + 1) * T, W:2 * W] = feature
    k_own = jnp.concatenate([kv[0, c, x, 0:T, 0:W], own_docs.astype(BF16)], axis=1)
    v_own = jnp.concatenate([kv[0, c, x, 0:T, W:2 * W], jnp.ones((T, W), BF16)], axis=1)
    causal = lax.broadcasted_iota(jnp.int32, (T, T), 0) >= lax.broadcasted_iota(jnp.int32, (T, T), 1)

    def diagonal(h):
        rows = slice(h * T, (h + 1) * T)
        scores = jnp.where(causal, dot_nt(qa[rows, :], k_own), -1e30)
        high = jnp.broadcast_to(jnp.max(scores, axis=1, keepdims=True) * SCALE, (T, W))
        weights = jnp.exp2(scores * SCALE - high[:, 0:1]).astype(BF16)
        top[rows, :] = high
        acc[rows, :] = jnp.dot(weights, v_own, preferred_element_type=F32)

    def attend(blocks, valid):
        for b in range(8):
            docs_b = doc_rows(kv[blocks[b], b // 4, b % 4, T:KVR, 0:W])
            ff[b] = jnp.where(valid[b], docs_b, 1.0).astype(BF16)
        half = HEADS * T // 2
        for u in range(2):
            rows = slice(u * half, (u + 1) * half)
            keys = jnp.concatenate([kv[blocks[b], b // 4, b % 4, 0:T, 0:W] for b in range(8)], axis=0)
            keys = jnp.concatenate([keys, ff[...].reshape(8 * T, W)], axis=1)
            scores = dot_nt(qa[rows, :], keys)
            old = top[rows, :]
            new = jnp.maximum(old, jnp.max(scores, axis=1, keepdims=True) * SCALE)
            weights = jnp.exp2(scores * SCALE - new[:, 0:1]).astype(BF16)
            vals = jnp.concatenate([kv[blocks[b], b // 4, b % 4, 0:T, W:2 * W] for b in range(8)], axis=0)
            vals = jnp.concatenate([vals, jnp.ones((8 * T, W), BF16)], axis=1)
            keep = jnp.exp2(old - new)
            acc[rows, :] = acc[rows, :] * jnp.concatenate([keep, keep], axis=1) + jnp.dot(
                weights, vals, preferred_element_type=F32)
            top[rows, :] = new

    def attend_plane(p):
        sib_wait(p)
        attend([p] * 8, [z >= p] * 8)

    z_step(1)
    diagonal(0)
    diagonal(1)
    z_step(2)
    x_end(1)
    diagonal(2)
    diagonal(3)
    z_step(3)
    diagonal(4)
    z_step(4)
    for i in (5, 6, 7):
        w_send(i)
    x_end(2)
    attend_plane(1)
    x_end(3)
    attend_plane(2)
    x_end(0)
    attend_plane(3)
    for i in (1, 2, 3):
        w_recv(i)
    sib_wait(0)
    early = [(b % 4) * 2 + b // 4 < me for b in range(8)]
    attend([jnp.where(e, 0, 4) for e in early], [e | (z >= 4) for e in early])

    for h in range(HEADS):
        rows = slice(h * T, (h + 1) * T)
        ag[x, :, h * W:(h + 1) * W] = (acc[rows, 0:W] / acc[rows, W:2 * W]).astype(BF16)
    lo, hi = pl.ds(0, 96), pl.ds(96, 96)
    go(rc(ag.at[x, lo], ax_s.at[0], ax_r.at[0], right))
    go(rc(ag.at[x, hi], ax_s.at[2], ax_r.at[2], left))
    go(rc(ag.at[x, hi], ax_s.at[1], ax_r.at[1], right))
    go(rc(ag.at[x, lo], ax_s.at[3], ax_r.at[3], left))

    for i in (5, 6, 7, 4):
        w_recv(i)
    wr[...] = jnp.zeros_like(wr)
    for i in range(NZ):
        plane = lax.rem(z + i, NZ)
        rc(wz.at[plane, oc], wd_s.at[i], wd_r.at[i], sib).wait_recv()
    for o in range(NY):
        wr[o, 96:112, :] = wz[o, 0, 64:80, :]
        wr[o, 112:128, :] = wz[o, 1, 64:80, :]

    def partial(j, o):
        xx = lax.rem(x + j, NX)
        cols = jnp.concatenate([wz[o, 0, 0:64, :], wz[o, 1, 0:64, :]], axis=0)
        main = dot_nt(ag[xx], cols)
        rest = dot_nt(ag[xx, 0:GROUP, :], wr[o, 96:224, :])
        for g in range(1, 4):
            rest += dot_nt(ag[xx, g * GROUP:(g + 1) * GROUP, :], wr[o, 96 - 32 * g:224 - 32 * g, :])
        return jnp.concatenate([main, rest], axis=0)

    y_up, y_down = dev(dy=1), dev(dy=-1)

    def hops(d, j):
        return 4 if (d + j) % 2 == 1 else 3

    def rs(d, r, j):
        return pltpu.make_async_remote_copy(
            src_ref=sbuf.at[d, r - 1, j], dst_ref=rbuf.at[d, r - 1, j],
            send_sem=rs_s.at[d, r - 1, j], recv_sem=rs_r.at[d, r - 1, j],
            device_id=y_up if d == 0 else y_down, device_id_type=MESH)

    def send_step(n, j):
        for d in range(2):
            r = hops(d, j) - n
            if r < 1:
                continue
            o = lax.rem(t + r, NY) if d == 0 else lax.rem(t - r + NY, NY)
            total = partial(j, o)
            if n > 0:
                rs(d, r + 1, j).wait_recv()
                total = total + rbuf[d, r, j].astype(F32)
            sbuf[d, r - 1, j] = total.astype(BF16)
            go(rs(d, r, j))

    def fx(j):
        return pltpu.make_async_remote_copy(
            src_ref=fsend.at[j - 1], dst_ref=fin.at[x], send_sem=fx_s.at[j - 1], recv_sem=fx_r.at[j - 1],
            device_id=dev(dx=j), device_id_type=MESH)

    def finish(j):
        total = partial(j, t)
        for d in range(2):
            rs(d, 1, j).wait_recv()
            total = total + rbuf[d, 0, j].astype(F32)
        if j == 0:
            fin[x] = total.astype(BF16)
        else:
            fsend[j - 1] = total.astype(BF16)
            go(fx(j))

    send_step(0, 0)
    rc(ag.at[xl, lo], ax_s.at[0], ax_r.at[0], right).wait_recv()
    go(rc(ag.at[xl, lo], ax_s.at[4], ax_r.at[4], right))
    rc(ag.at[xr, hi], ax_s.at[2], ax_r.at[2], left).wait_recv()
    go(rc(ag.at[xr, hi], ax_s.at[5], ax_r.at[5], left))
    send_step(1, 0)

    r5 = lax.broadcasted_iota(jnp.int32, (NX * W, K), 0)
    col = lax.broadcasted_iota(jnp.int32, (NX * W, K), 1)
    part, lane = r5 // W, lax.rem(r5, W)
    selm[...] = jnp.where(col == part * 160 + lane + jnp.where(lane < 64, 0, 16), 1.0, 0.0).astype(BF16)
    spot = lax.rem(lane, 32)
    goal = part * 160 + spot + jnp.where(spot < 16, 64, 128)
    for g in range(4):
        selr[g] = jnp.where((col == goal) & (lane // 32 == g), 1.0, 0.0).astype(BF16)

    rc(ag.at[xl, hi], ax_s.at[1], ax_r.at[1], right).wait_recv()
    rc(ag.at[xr, lo], ax_s.at[3], ax_r.at[3], left).wait_recv()
    send_step(0, 1)
    send_step(0, 3)
    send_step(2, 0)
    rc(ag.at[xo, lo], ax_s.at[4], ax_r.at[4], right).wait_recv()
    rc(ag.at[xo, hi], ax_s.at[5], ax_r.at[5], left).wait_recv()
    send_step(0, 2)
    send_step(1, 1)
    send_step(1, 3)
    send_step(3, 0)
    send_step(1, 2)
    send_step(2, 1)
    send_step(2, 3)
    finish(0)
    send_step(2, 2)
    send_step(3, 1)
    send_step(3, 3)
    send_step(3, 2)
    finish(1)
    finish(3)
    finish(2)
    for j in (1, 3, 2):
        pltpu.make_async_remote_copy(
            src_ref=fsend.at[j - 1], dst_ref=fin.at[lax.rem(x - j + NX, NX)], send_sem=fx_s.at[j - 1],
            recv_sem=fx_r.at[j - 1], device_id=dev(dx=j), device_id_type=MESH).wait_recv()

    main = jnp.concatenate([fin[i, 0:T, :] for i in range(NX)], axis=1)
    rest = jnp.concatenate([fin[i, T:PACK, :] for i in range(NX)], axis=1)
    for g in range(4):
        rows = slice(g * GROUP, (g + 1) * GROUP)
        o_ref[rows, :] = (
            jnp.dot(main[rows, :], selm[...], preferred_element_type=F32)
            + jnp.dot(rest, selr[g], preferred_element_type=F32)).astype(BF16)

    for copy, cond in started:
        if cond is None:
            copy.wait_send()
        else:
            pl.when(cond)(copy.wait_send)


def local(queries, keys, values, doc_ids, w_out):
    sem = pltpu.SemaphoreType.DMA
    vmem = pl.BlockSpec(memory_space=pltpu.VMEM)
    return pl.pallas_call(
        kernel,
        out_shape=jax.ShapeDtypeStruct((T, K), BF16),
        in_specs=[pl.BlockSpec(memory_space=pl.ANY)] * 5,
        out_specs=vmem,
        scratch_shapes=[
            pltpu.VMEM((DEPTH, 2, NX, KVR, 2 * W), BF16),
            pltpu.VMEM((8, T, W), BF16),
            pltpu.VMEM((T, K), BF16),
            pltpu.VMEM((1, T), jnp.int32),
            pltpu.VMEM((HEADS * T, 2 * W), BF16),
            pltpu.VMEM((HEADS * T, 2 * W), F32),
            pltpu.VMEM((HEADS * T, W), F32),
            pltpu.VMEM((NZ, 2, COLS, K), BF16),
            pltpu.VMEM((NY, 224, K), BF16),
            pltpu.VMEM((NX, T, K), BF16),
            pltpu.VMEM((2, 4, NX, PACK, W), BF16),
            pltpu.VMEM((2, 4, NX, PACK, W), BF16),
            pltpu.VMEM((3, PACK, W), BF16),
            pltpu.VMEM((NX, PACK, W), BF16),
            pltpu.VMEM((NX * W, K), BF16),
            pltpu.VMEM((4, NX * W, K), BF16),
            sem((5,)), sem((4, 2)), sem((4, 2)), sem((5, 3)), sem((5, 3)), sem((5, 4)), sem((5, 4)),
            sem((8,)), sem((8,)), sem((8,)), sem((8,)),
            sem((6,)), sem((6,)), sem((2, 4, NX)), sem((2, 4, NX)), sem((3,)), sem((3,)),
        ],
        compiler_params=pltpu.CompilerParams(
            collective_id=0, has_side_effects=True, vmem_limit_bytes=56 * 2**20),
        name="attend_project",
    )(queries, keys, values, doc_ids.reshape(1, T), w_out.T)


def solution(mesh):
    placed = (P("seq", "tp"), P("seq", "tp"), P("seq", "tp"), P("seq"), P("tp", "seq"))
    return jax.shard_map(
        local, mesh=mesh, in_specs=placed, out_specs=P("seq", "tp"), check_vma=False
    )
```

time: 105 us -> 87.2 us (0.83); the launches traced: 105 us -> 85.8 us
  Pallas kernels: 104 us -> 84.1 us
    pallas_call x1, Pallas kernels: 104 us -> 84.1 us  [local(): pl.pallas_call(kernel, out_shape=jax.ShapeDtypeStruct((T, K), BF16), in_s...]
where the time goes in v2:
time: 87.2 us; the launch traced here: 85.8 us
  Pallas kernels  84.1 us (96%)
  local copies, waits for them, and re-layouts  1.66 us (2%)
    pallas_call x1, Pallas kernels, local(): pl.pallas_call(kernel, out_shape=jax.ShapeDtypeStruct((T, K), BF16), in_s...  84.1 us

profile of v2, /device:TPU:6, one launch (start us, length us, event | category | flops | bytes accessed | tf_op | source)
XLA Modules:
  0.0 85.8 jit_solution(7108171735905264763)
XLA Ops:
  0.0 84.1 %attend_project.1 = bf16[192,640]{1,0:T(8,128)(2,1)} custom-call(bf16[192,640]{1,0:T(8,128)(2,1)} %q_hbm.1, bf16[192,128]{1,0:T(8,128)(2,1)} %k_hbm.1, bf16[192,128]{1,0:T(8,128)(2,1)} %v_hbm.1, s32[1,192]{1,0:T(1,128)} %bitcast.3, bf16[80,640]{1,0:T(8,128)(2,1)} %bitcast.2), custom_call_target="tpu_custom_call" | custom-call | tf_op jit(solution)/shard_map/attend_project/pallas_call | solution.py:362
  84.2 1.7 %copy.7 = bf16[192,640]{1,0:T(8,128)(2,1)} copy(bf16[192,640]{1,0:T(8,128)(2,1)} %attend_project.1) | data formatting | bytes 491520

commit v3 on v2

v3 whole, which is shorter than its diff:
```python
import functools
import math

import jax
import jax.numpy as jnp
from jax import lax
from jax.experimental import pallas as pl
from jax.experimental.pallas import tpu as pltpu
from jax.sharding import PartitionSpec as P

MESH = pl.DeviceIdType.MESH
F32, BF16 = jnp.float32, jnp.bfloat16
NT = (((1,), (1,)), ((), ()))

NZ, NX, NY = 8, 4, 8
T = 192
HEADS = 5
W = 128
STAT = 16
KVR = T + STAT
DEPTH = 5
COLS = 80
K = HEADS * W
HALF = T // 2
GROUP = 48
PACK = T + GROUP
SCALE = math.log2(math.e) / math.sqrt(W)
HIDE = -131072.0


def dot_nt(a, b):
    return lax.dot_general(a, b, NT, preferred_element_type=F32)


def kernel(q_hbm, k_hbm, v_hbm, d_hbm, w_hbm, o_ref,
           kv, ff, qv, dv, qa, acc, top, wz, wr, ag, sbuf, rbuf, fsend, fin, selm, selr,
           in_s, kvz_s, kvz_r, kvx_s, kvx_r, kvm_s, kvm_r, kvd_s, kvd_r, wz_s, wz_r, wd_s, wd_r,
           ax_s, ax_r, rs_s, rs_r, fx_s, fx_r):
    s = lax.axis_index("seq")
    t = lax.axis_index("tp")
    z, x, c = s // 8, lax.rem(s // 2, 4), lax.rem(s, 2)
    me = x * 2 + c

    def dev(dz=0, dx=0, dc=0, dy=0):
        zz = lax.rem(z + dz + NZ, NZ)
        xx = lax.rem(x + dx + NX, NX)
        cc = lax.rem(c + dc, 2)
        return (zz * 8 + xx * 2 + cc, lax.rem(t + dy + NY, NY))

    up, right, left, across = dev(dz=1), dev(dx=1), dev(dx=-1), dev(dx=2)
    sib = dev(dc=1)
    xr, xl, xo = lax.rem(x + 1, NX), lax.rem(x + 3, NX), lax.rem(x + 2, NX)
    oc = 1 - c

    def rc(ref, ss, rs, to):
        return pltpu.make_async_remote_copy(
            src_ref=ref, dst_ref=ref, send_sem=ss, recv_sem=rs, device_id=to, device_id_type=MESH)

    barrier = pltpu.get_barrier_semaphore()
    peers = [dev(dz=i) for i in (1, -1, 2, -2)] + [right, left, across, sib] + [dev(dy=i) for i in (1, -1, 2, -2)]
    for peer in peers:
        pl.semaphore_signal(barrier, inc=1, device_id=peer, device_id_type=MESH)
    loads = [
        pltpu.make_async_copy(d_hbm, dv, in_s.at[0]),
        pltpu.make_async_copy(k_hbm, kv.at[0, c, x, pl.ds(0, T), pl.ds(0, W)], in_s.at[1]),
        pltpu.make_async_copy(v_hbm, kv.at[0, c, x, pl.ds(0, T), pl.ds(W, W)], in_s.at[2]),
        pltpu.make_async_copy(w_hbm, wz.at[z, c], in_s.at[3]),
        pltpu.make_async_copy(q_hbm, qv, in_s.at[4]),
    ]
    for load in loads:
        load.start()

    loads[0].wait()
    docs = jnp.broadcast_to(dv[...], (W, T))
    number = lax.broadcasted_iota(jnp.int32, (W, T), 0)
    first = jnp.sum((docs < number).astype(F32), axis=1, keepdims=True)
    last = jnp.sum((docs <= number).astype(F32), axis=1, keepdims=True)
    first = jnp.transpose(jnp.broadcast_to(first, (W, W)))
    last = jnp.transpose(jnp.broadcast_to(last, (W, W)))
    stat = jnp.concatenate([first[0:8], last[0:8]], axis=0).astype(BF16)
    kv[0, c, x, T:KVR, 0:W] = stat
    kv[0, c, x, T:KVR, W:2 * W] = jnp.zeros((STAT, W), BF16)
    loads[1].wait()
    loads[2].wait()

    pl.semaphore_wait(barrier, len(peers))

    started = []

    def go(copy):
        copy.start()
        started.append((copy, None))

    def go_if(cond, copy):
        @pl.when(cond)
        def _():
            copy.start()
        started.append((copy, cond))

    def z_copy(p, half):
        rows = pl.ds(0, 96) if half == 0 else pl.ds(96, KVR - 96)
        return pltpu.make_async_remote_copy(
            src_ref=kv.at[p, c, x, rows], dst_ref=kv.at[p + 1, c, x, rows], send_sem=kvz_s.at[p, half],
            recv_sem=kvz_r.at[p, half], device_id=up, device_id_type=MESH)

    def x_start(p):
        blk = kv.at[p, c, x]
        go(rc(blk, kvx_s.at[p, 0], kvx_r.at[p, 0], right))
        go(rc(blk, kvx_s.at[p, 1], kvx_r.at[p, 1], left))
        go(rc(blk, kvd_s.at[p, 0], kvd_r.at[p, 0], sib))

    low, high = pl.ds(0, 96), pl.ds(96, KVR - 96)

    def x_relay(p):
        ref = kv.at[p, c, xl]
        rc(ref, kvx_s.at[p, 0], kvx_r.at[p, 0], right).wait_recv()
        go(rc(kv.at[p, c, xl, low], kvx_s.at[p, 2], kvx_r.at[p, 2], right))
        go(rc(ref, kvd_s.at[p, 1], kvd_r.at[p, 1], sib))
        ref = kv.at[p, c, xr]
        rc(ref, kvx_s.at[p, 1], kvx_r.at[p, 1], left).wait_recv()
        go(rc(kv.at[p, c, xr, high], kvx_s.at[p, 3], kvx_r.at[p, 3], left))
        go(rc(ref, kvd_s.at[p, 2], kvd_r.at[p, 2], sib))

    def x_end(p):
        rc(kv.at[p, c, xo, low], kvx_s.at[p, 2], kvx_r.at[p, 2], right).wait_recv()
        rc(kv.at[p, c, xo, high], kvx_s.at[p, 3], kvx_r.at[p, 3], left).wait_recv()
        go(rc(kv.at[p, c, xo], kvd_s.at[p, 3], kvd_r.at[p, 3], sib))

    def x_start_mixed(p, half):
        rows = (low, high)[half]
        for i, (to, dest) in enumerate(((right, xr), (left, xl), (across, xo))):
            go_if((x < dest) if p == 0 else (x > dest),
                  rc(kv.at[p, c, x, rows], kvm_s.at[p // 4, half, i], kvm_r.at[half, i], to))
        if half == 1:
            go_if(c == (0 if p == 0 else 1), rc(kv.at[p, c, x], kvd_s.at[p, 0], kvd_r.at[0, 0], sib))

    def plane_of(p, xx):
        return p if p > 0 else jnp.where(xx < x, 0, 4)

    def x_end_mixed():
        for i, xx in enumerate((xl, xr, xo)):
            ref = kv.at[plane_of(0, xx), c, xx]
            for half, rows in enumerate((low, high)):
                rc(ref.at[rows], kvm_s.at[0, half, i], kvm_r.at[half, i], right).wait_recv()
            go(rc(ref, kvd_s.at[0, i + 1], kvd_r.at[0, i + 1], sib))

    def sib_wait(p):
        own = p if p > 0 else jnp.where(c == 1, 0, 4)
        for i, (pp, xx) in enumerate(((own, x), (plane_of(p, xl), xl), (plane_of(p, xr), xr), (plane_of(p, xo), xo))):
            rc(kv.at[pp, oc, xx], kvd_s.at[p, i], kvd_r.at[p, i], sib).wait_recv()

    def z_step(p):
        for half in range(2):
            z_copy(p - 1, half).wait_recv()
            if p < DEPTH - 1:
                go(z_copy(p, half))
            else:
                x_start_mixed(p, half)
        if p < DEPTH - 1:
            x_start(p)

    def w_send(offset, i, dz):
        go(rc(wz.at[lax.rem(z + offset, NZ), c], wz_s.at[i], wz_r.at[i], dev(dz=dz)))

    def w_recv(i):
        ref = wz.at[lax.rem(z + i, NZ), c]
        rc(ref, wz_s.at[i], wz_r.at[i], up).wait_recv()
        go(rc(ref, wd_s.at[i], wd_r.at[i], sib))

    go(z_copy(0, 0))
    go(z_copy(0, 1))
    x_start_mixed(0, 0)
    x_start_mixed(0, 1)
    loads[3].wait()
    w_send(0, 1, -1)
    w_send(0, 2, -2)
    go(rc(wz.at[z, c], wd_s.at[0], wd_r.at[0], sib))

    row = lax.broadcasted_iota(jnp.int32, (T, W), 0).astype(F32)

    def doc_rows(bounds):
        bounds = bounds.astype(F32)
        return jnp.where((row >= bounds[0:1]) & (row < bounds[8:9]), 1.0, 0.0)

    own_docs = doc_rows(stat)
    feature = jnp.where(own_docs > 0.5, 0.0, HIDE).astype(BF16)
    loads[4].wait()
    for u in range(2):
        for h in range(HEADS):
            rows = slice((u * HEADS + h) * HALF, (u * HEADS + h + 1) * HALF)
            qa[rows, 0:W] = qv[u * HALF:(u + 1) * HALF, h * W:(h + 1) * W]
            qa[rows, W:2 * W] = feature[u * HALF:(u + 1) * HALF]
    k_own = jnp.concatenate([kv[0, c, x, 0:T, 0:W], own_docs.astype(BF16)], axis=1)
    v_own = jnp.concatenate([kv[0, c, x, 0:T, W:2 * W], jnp.ones((T, W), BF16)], axis=1)
    wr[...] = jnp.zeros_like(wr)

    def diagonal(u):
        rows = slice(u * HEADS * HALF, (u + 1) * HEADS * HALF)
        at = lax.broadcasted_iota(jnp.int32, (HALF, T), 0) + u * HALF
        causal = at >= lax.broadcasted_iota(jnp.int32, (HALF, T), 1)
        scores = jnp.where(jnp.concatenate([causal] * HEADS, axis=0), dot_nt(qa[rows, :], k_own), -1e30)
        high = jnp.broadcast_to(jnp.max(scores, axis=1, keepdims=True) * SCALE, (HEADS * HALF, W))
        weights = jnp.exp2(scores * SCALE - high[:, 0:1]).astype(BF16)
        top[rows, :] = high
        acc[rows, :] = jnp.dot(weights, v_own, preferred_element_type=F32)

    def attend(blocks, valid, tile, after=None):
        count = len(blocks)
        for i, where in enumerate(blocks):
            docs_b = doc_rows(kv[where[0], where[1], where[2], T:KVR, 0:W])
            ff[i] = jnp.where(valid[i], docs_b, 1.0).astype(BF16)

        def score(u):
            keys = jnp.concatenate([kv[i[0], i[1], i[2], 0:T, 0:W] for i in blocks], axis=0)
            keys = jnp.concatenate([keys, ff[0:count].reshape(count * T, W)], axis=1)
            return dot_nt(qa[u * tile:(u + 1) * tile, :], keys)

        tiles = HEADS * T // tile
        ahead = score(0)
        for u in range(tiles):
            rows = slice(u * tile, (u + 1) * tile)
            scores = ahead
            if u + 1 < tiles:
                ahead = score(u + 1)
            old = top[rows, :]
            new = jnp.maximum(old, jnp.max(scores, axis=1, keepdims=True) * SCALE)
            weights = jnp.exp2(scores * SCALE - new[:, 0:1]).astype(BF16)
            vals = jnp.concatenate([kv[i[0], i[1], i[2], 0:T, W:2 * W] for i in blocks], axis=0)
            vals = jnp.concatenate([vals, jnp.ones((count * T, W), BF16)], axis=1)
            keep = jnp.exp2(old - new)
            acc[rows, :] = acc[rows, :] * jnp.concatenate([keep, keep], axis=1) + jnp.dot(
                weights, vals, preferred_element_type=F32)
            top[rows, :] = new
            if after is not None:
                after(u)

    def attend_plane(p):
        sib_wait(p)
        attend([(p, b // 4, b % 4) for b in range(8)], [z >= p] * 8, 320)

    def attend_mixed(core, after=None):
        early = [i * 2 + core < me for i in range(NX)]
        attend([(jnp.where(e, 0, 4), core, i) for i, e in enumerate(early)], [e | (z >= 4) for e in early], 480, after)

    def a_send(u):
        mine = slice(u * HALF, (u + 1) * HALF)
        for h in range(HEADS):
            rows = slice((u * HEADS + h) * HALF, (u * HEADS + h + 1) * HALF)
            ag[0, mine, h * W:(h + 1) * W] = (acc[rows, 0:W] / acc[rows, W:2 * W]).astype(BF16)
        for i, to in enumerate((right, left)):
            go(pltpu.make_async_remote_copy(
                src_ref=ag.at[0, pl.ds(u * HALF, HALF)], dst_ref=ag.at[1 + u, pl.ds(i * HALF, HALF)],
                send_sem=ax_s.at[u, i], recv_sem=ax_r.at[u, i], device_id=to, device_id_type=MESH))

    def a_far_copy(u, i):
        return pltpu.make_async_remote_copy(
            src_ref=ag.at[1 + u, pl.ds(i * (HALF + GROUP), GROUP)],
            dst_ref=ag.at[3, pl.ds(u * HALF + i * GROUP, GROUP)],
            send_sem=ax_s.at[u, 2 + i], recv_sem=ax_r.at[u, 2 + i],
            device_id=(right, left)[i], device_id_type=MESH)

    def a_near(u):
        for i in range(2):
            rc(ag.at[1 + u, pl.ds(i * HALF, HALF)], ax_s.at[u, i], ax_r.at[u, i], right).wait_recv()
            go(a_far_copy(u, i))

    def a_far():
        for u in range(2):
            for i in range(2):
                a_far_copy(u, i).wait_recv()

    def w_ready(i):
        plane = lax.rem(z + i, NZ)
        rc(wz.at[plane, oc], wd_s.at[i], wd_r.at[i], sib).wait_recv()
        for g in range(4):
            wr[plane, 32 * g:32 * g + 16, g * K:(g + 1) * K] = wz[plane, 0, 64:80, :]
            wr[plane, 32 * g + 16:32 * g + 32, g * K:(g + 1) * K] = wz[plane, 1, 64:80, :]

    z_step(1)
    diagonal(0)
    z_step(2)
    x_relay(1)
    z_step(3)
    w_send(0, 7, 1)
    w_send(0, 6, 2)
    diagonal(1)
    x_end(1)
    x_relay(2)
    w_recv(2)
    w_send(2, 3, -1)
    w_send(2, 4, -2)
    attend_plane(1)
    z_step(4)
    x_end(2)
    x_relay(3)
    attend_plane(2)
    x_end(3)
    w_recv(6)
    w_send(6, 5, 1)
    attend_plane(3)
    x_end_mixed()
    for i in (1, 7, 3, 4):
        w_recv(i)
    attend_mixed(c)
    w_recv(5)
    for i in (0, 1, 2, 3, 4, 6, 7):
        w_ready(i)
    sib_wait(0)
    attend_mixed(oc, a_send)
    w_ready(5)

    def partial(j, o):
        cols = jnp.concatenate([wz[o, 0, 0:64, :], wz[o, 1, 0:64, :]], axis=0)
        main = dot_nt(ag[j], cols)
        rows = jnp.concatenate([ag[j, g * GROUP:(g + 1) * GROUP, :] for g in range(4)], axis=1)
        rest = dot_nt(rows, wr[o])
        return jnp.concatenate([main[0:HALF], rest, main[HALF:T]], axis=0)

    y_up, y_down = dev(dy=1), dev(dy=-1)

    def hops(d, j):
        return 4 if (d + j) % 2 == 1 else 3

    def rs(d, r, j):
        leap = 2 if (j == 3 and r == 4) else 1
        return pltpu.make_async_remote_copy(
            src_ref=sbuf.at[d, r - 1, j], dst_ref=rbuf.at[d, r - 1, j],
            send_sem=rs_s.at[d, r - 1, j], recv_sem=rs_r.at[d, r - 1, j],
            device_id=dev(dy=leap if d == 0 else -leap), device_id_type=MESH)

    def send_block(d, r, j, arrived):
        total = partial(j, lax.rem(t + r, NY) if d == 0 else lax.rem(t - r + NY, NY))
        for i in arrived:
            rs(d, i, j).wait_recv()
            total = total + rbuf[d, i - 1, j].astype(F32)
        sbuf[d, r - 1, j] = total.astype(BF16)
        go(rs(d, r, j))

    def send_step(n, j):
        for d in range(2):
            if j == 3 and hops(d, j) == 4:
                if n == 0:
                    send_block(d, 4, j, ())
                r = 3 - n
                arrived = () if n == 0 else (4, 3) if n == 1 else (2,)
            else:
                r = hops(d, j) - n
                arrived = () if n == 0 else (r + 1,)
            if r > 0:
                send_block(d, r, j, arrived)

    def fx(j, i):
        to, slot, half = ((), ((left, 1, 0), (right, 3, 0)), ((left, 1, 1), (right, 3, 1)), ((across, 2, 0), (across, 2, 1)))[j][i]
        return pltpu.make_async_remote_copy(
            src_ref=fsend.at[j - 1, pl.ds(i * HALF, HALF + GROUP)], dst_ref=fin.at[slot, half],
            send_sem=fx_s.at[2 * slot + half - 2], recv_sem=fx_r.at[2 * slot + half - 2],
            device_id=to, device_id_type=MESH)

    def finish(j):
        total = partial(j, t)
        for d in range(2):
            rs(d, 1, j).wait_recv()
            total = total + rbuf[d, 0, j].astype(F32)
        total = total.astype(BF16)
        if j == 0:
            fin[0, 0] = total[0:HALF + GROUP]
            fin[0, 1] = total[HALF:PACK]
        else:
            fsend[j - 1] = total
            go(fx(j, 0))
            go(fx(j, 1))

    def second(slot, half):
        return slot == 3 or (slot != 1 and half == 1)

    send_step(0, 0)
    a_near(0)
    send_step(0, 1)

    lane = lax.broadcasted_iota(jnp.int32, (W, K), 0)
    spot = lax.rem(lane, 32)
    main_at = lane + jnp.where(lane < 64, 0, 16)
    rest_at = spot + jnp.where(spot < 16, 64, 128)
    for i in range(NX):
        col = lax.broadcasted_iota(jnp.int32, (W, K), 1) - lax.rem(x + i, NX) * 160
        rows = slice(i * W, (i + 1) * W)
        selm[rows, :] = jnp.where(col == main_at, 1.0, 0.0).astype(BF16)
        for u in range(2):
            for g in range(2):
                here = lane // 32 == g + (2 if second(i, u) else 0)
                selr[2 * u + g, rows, :] = jnp.where((col == rest_at) & here, 1.0, 0.0).astype(BF16)

    send_step(1, 0)
    a_near(1)
    send_step(0, 2)
    send_step(1, 1)
    send_step(2, 0)
    a_far()
    send_step(0, 3)
    send_step(1, 2)
    send_step(2, 1)
    send_step(1, 3)
    send_step(2, 2)
    send_step(3, 1)
    send_step(2, 3)
    send_step(3, 2)
    send_step(3, 0)
    finish(1)
    finish(2)
    finish(3)
    finish(0)
    for j in (1, 2, 3):
        for i in range(2):
            fx(j, i).wait_recv()

    def main_of(i, u):
        return fin[i, u, GROUP:GROUP + HALF, :] if second(i, u) else fin[i, u, 0:HALF, :]

    def rest_of(i, u):
        return fin[i, u, 0:GROUP, :] if second(i, u) else fin[i, u, HALF:HALF + GROUP, :]

    for u in range(2):
        main = jnp.dot(jnp.concatenate([main_of(i, u) for i in range(NX)], axis=1), selm[...], preferred_element_type=F32)
        rest = jnp.concatenate([rest_of(i, u) for i in range(NX)], axis=1)
        for g in range(2):
            add = jnp.dot(rest, selr[2 * u + g], preferred_element_type=F32)
            o_ref[u * HALF + g * GROUP:u * HALF + (g + 1) * GROUP, :] = (
                main[g * GROUP:(g + 1) * GROUP] + add).astype(BF16)

    for copy, cond in started:
        if cond is None:
            copy.wait_send()
        else:
            pl.when(cond)(copy.wait_send)


def local(queries, keys, values, doc_ids, w_out):
    sem = pltpu.SemaphoreType.DMA
    vmem = pl.BlockSpec(memory_space=pltpu.VMEM)
    return pl.pallas_call(
        kernel,
        out_shape=pltpu.VMEM((T, K), BF16),
        in_specs=[pl.BlockSpec(memory_space=pl.ANY)] * 5,
        out_specs=vmem,
        scratch_shapes=[
            pltpu.VMEM((DEPTH, 2, NX, KVR, 2 * W), BF16),
            pltpu.VMEM((8, T, W), BF16),
            pltpu.VMEM((T, K), BF16),
            pltpu.VMEM((1, T), jnp.int32),
            pltpu.VMEM((HEADS * T, 2 * W), BF16),
            pltpu.VMEM((HEADS * T, 2 * W), F32),
            pltpu.VMEM((HEADS * T, W), F32),
            pltpu.VMEM((NZ, 2, COLS, K), BF16),
            pltpu.VMEM((NY, W, 4 * K), BF16),
            pltpu.VMEM((NX, T, K), BF16),
            pltpu.VMEM((2, 4, NX, PACK, W), BF16),
            pltpu.VMEM((2, 4, NX, PACK, W), BF16),
            pltpu.VMEM((3, PACK, W), BF16),
            pltpu.VMEM((NX, 2, HALF + GROUP, W), BF16),
            pltpu.VMEM((NX * W, K), BF16),
            pltpu.VMEM((4, NX * W, K), BF16),
            sem((5,)), sem((4, 2)), sem((4, 2)), sem((4, 4)), sem((4, 4)), sem((2, 2, 3)), sem((2, 3)), sem((5, 4)), sem((5, 4)),
            sem((8,)), sem((8,)), sem((8,)), sem((8,)),
            sem((2, 4)), sem((2, 4)), sem((2, 4, NX)), sem((2, 4, NX)), sem((6,)), sem((6,)),
        ],
        compiler_params=pltpu.CompilerParams(
            collective_id=0, has_side_effects=True, vmem_limit_bytes=56 * 2**20),
        name="attend_project",
    )(queries, keys, values, doc_ids.reshape(1, T), w_out.T)


def solution(mesh):
    placed = (P("seq", "tp"), P("seq", "tp"), P("seq", "tp"), P("seq"), P("tp", "seq"))
    return jax.shard_map(
        local, mesh=mesh, in_specs=placed, out_specs=P("seq", "tp"), check_vma=False
    )
```

time: 87.2 us -> 81.9 us (0.939)
  Pallas kernels: 84.1 us -> 79.8 us
  local copies, waits for them, and re-layouts: 1.66 us -> 0.7 us
    pallas_call x1, Pallas kernels: 84.1 us -> 79.8 us  [local(): pl.pallas_call(kernel, out_shape=pltpu.VMEM((T, K), BF16), in_specs=[pl.B...]
    unnamed x1, local copies, waits for them, and re-layouts: 1.66 us -> 0.7 us
where the time goes in v3:
time: 81.9 us; the launch traced here: 80.5 us
  Pallas kernels  79.8 us (97%)
    pallas_call x1, Pallas kernels, local(): pl.pallas_call(kernel, out_shape=pltpu.VMEM((T, K), BF16), in_specs=[pl.B...  79.8 us

profile of v3, /device:TPU:6, one launch (start us, length us, event | category | flops | bytes accessed | tf_op | source)
XLA Modules:
  0.0 80.5 jit_solution(11757086847229253222)
XLA Ops:
  0.0 79.8 %attend_project.1 = bf16[192,640]{1,0:T(8,128)(2,1)S(1)} custom-call(bf16[192,640]{1,0:T(8,128)(2,1)} %q_hbm.1, bf16[192,128]{1,0:T(8,128)(2,1)} %k_hbm.1, bf16[192,128]{1,0:T(8,128)(2,1)} %v_hbm.1, s32[1,192]{1,0:T(1,128)} %bitcast.3, bf16[80,640]{1,0:T(8,128)(2,1)} %bitcast.2), custom_call_target="tpu_custom_call" | custom-call | tf_op jit(solution)/shard_map/attend_project/pallas_call | solution.py:440
  79.8 0.7 copy.7

commit v4 on v3

--- a/solution.py
+++ b/solution.py
@@ -33,7 +33,7 @@
 
 
 def kernel(q_hbm, k_hbm, v_hbm, d_hbm, w_hbm, o_ref,
-           kv, ff, qv, dv, qa, acc, top, wz, wr, ag, sbuf, rbuf, fsend, fin, selm, selr,
+           kv, ff, qv, dv, qa, acc, top, wz, wr, ag, sbuf, rbuf, fsend, fin, selm, selr, out,
            in_s, kvz_s, kvz_r, kvx_s, kvx_r, kvm_s, kvm_r, kvd_s, kvd_r, wz_s, wz_r, wd_s, wd_r,
            ax_s, ax_r, rs_s, rs_r, fx_s, fx_r):
     s = lax.axis_index("seq")
@@ -70,6 +70,96 @@
     for load in loads:
         load.start()
 
+    loads[1].wait()
+    loads[2].wait()
+
+    pl.semaphore_wait(barrier, len(peers))
+
+    started = []
+
+    def go(copy):
+        copy.start()
+        started.append((copy, None))
+
+    def go_if(cond, copy):
+        @pl.when(cond)
+        def _():
+            copy.start()
+        started.append((copy, cond))
+
+    def z_copy(p, half):
+        rows = pl.ds(0, 96) if half == 0 else pl.ds(96, KVR - 96)
+        return pltpu.make_async_remote_copy(
+            src_ref=kv.at[p, c, x, rows], dst_ref=kv.at[p + 1, c, x, rows], send_sem=kvz_s.at[p, half],
+            recv_sem=kvz_r.at[p, half], device_id=up, device_id_type=MESH)
+
+    def x_start(p):
+        blk = kv.at[p, c, x]
+        go(rc(blk, kvx_s.at[p, 0], kvx_r.at[p, 0], right))
+        go(rc(blk, kvx_s.at[p, 1], kvx_r.at[p, 1], left))
+        go(rc(blk, kvd_s.at[p, 0], kvd_r.at[p, 0], sib))
+
+    low, high = pl.ds(0, 96), pl.ds(96, KVR - 96)
+
+    def x_relay(p):
+        ref = kv.at[p, c, xl]
+        rc(ref, kvx_s.at[p, 0], kvx_r.at[p, 0], right).wait_recv()
+        go(rc(kv.at[p, c, xl, low], kvx_s.at[p, 2], kvx_r.at[p, 2], right))
+        go(rc(ref, kvd_s.at[p, 1], kvd_r.at[p, 1], sib))
+        ref = kv.at[p, c, xr]
+        rc(ref, kvx_s.at[p, 1], kvx_r.at[p, 1], left).wait_recv()
+        go(rc(kv.at[p, c, xr, high], kvx_s.at[p, 3], kvx_r.at[p, 3], left))
+        go(rc(ref, kvd_s.at[p, 2], kvd_r.at[p, 2], sib))
+
+    def x_end(p):
+        rc(kv.at[p, c, xo, low], kvx_s.at[p, 2], kvx_r.at[p, 2], right).wait_recv()
+        rc(kv.at[p, c, xo, high], kvx_s.at[p, 3], kvx_r.at[p, 3], left).wait_recv()
+        go(rc(kv.at[p, c, xo], kvd_s.at[p, 3], kvd_r.at[p, 3], sib))
+
+    def x_start_mixed(p, half):
+        rows = (low, high)[half]
+        for i, (to, dest) in enumerate(((right, xr), (left, xl), (across, xo))):
+            go_if((x < dest) if p == 0 else (x > dest),
+                  rc(kv.at[p, c, x, rows], kvm_s.at[p // 4, half, i], kvm_r.at[half, i], to))
+        if half == 1:
+            go_if(c == (0 if p == 0 else 1), rc(kv.at[p, c, x], kvd_s.at[p, 0], kvd_r.at[0, 0], sib))
+
+    def plane_of(p, xx):
+        return p if p > 0 else jnp.where(xx < x, 0, 4)
+
+    def x_end_mixed():
+        for i, xx in enumerate((xl, xr, xo)):
+            ref = kv.at[plane_of(0, xx), c, xx]
+            for half, rows in enumerate((low, high)):
+                rc(ref.at[rows], kvm_s.at[0, half, i], kvm_r.at[half, i], right).wait_recv()
+            go(rc(ref, kvd_s.at[0, i + 1], kvd_r.at[0, i + 1], sib))
+
+    def sib_wait(p):
+        own = p if p > 0 else jnp.where(c == 1, 0, 4)
+        for i, (pp, xx) in enumerate(((own, x), (plane_of(p, xl), xl), (plane_of(p, xr), xr), (plane_of(p, xo), xo))):
+            rc(kv.at[pp, oc, xx], kvd_s.at[p, i], kvd_r.at[p, i], sib).wait_recv()
+
+    def z_step(p):
+        for half in range(2):
+            z_copy(p - 1, half).wait_recv()
+            if p < DEPTH - 1:
+                go(z_copy(p, half))
+            else:
+                x_start_mixed(p, half)
+        if p < DEPTH - 1:
+            x_start(p)
+
+    def w_send(offset, i, dz):
+        go(rc(wz.at[lax.rem(z + offset, NZ), c], wz_s.at[i], wz_r.at[i], dev(dz=dz)))
+
+    def w_recv(i):
+        ref = wz.at[lax.rem(z + i, NZ), c]
+        rc(ref, wz_s.at[i], wz_r.at[i], up).wait_recv()
+        go(rc(ref, wd_s.at[i], wd_r.at[i], sib))
+
+    go(z_copy(0, 0))
+    x_start_mixed(0, 0)
+
     loads[0].wait()
     docs = jnp.broadcast_to(dv[...], (W, T))
     number = lax.broadcasted_iota(jnp.int32, (W, T), 0)
@@ -80,96 +170,8 @@
     stat = jnp.concatenate([first[0:8], last[0:8]], axis=0).astype(BF16)
     kv[0, c, x, T:KVR, 0:W] = stat
     kv[0, c, x, T:KVR, W:2 * W] = jnp.zeros((STAT, W), BF16)
-    loads[1].wait()
-    loads[2].wait()
-
-    pl.semaphore_wait(barrier, len(peers))
-
-    started = []
-
-    def go(copy):
-        copy.start()
-        started.append((copy, None))
-
-    def go_if(cond, copy):
-        @pl.when(cond)
-        def _():
-            copy.start()
-        started.append((copy, cond))
-
-    def z_copy(p, half):
-        rows = pl.ds(0, 96) if half == 0 else pl.ds(96, KVR - 96)
-        return pltpu.make_async_remote_copy(
-            src_ref=kv.at[p, c, x, rows], dst_ref=kv.at[p + 1, c, x, rows], send_sem=kvz_s.at[p, half],
-            recv_sem=kvz_r.at[p, half], device_id=up, device_id_type=MESH)
-
-    def x_start(p):
-        blk = kv.at[p, c, x]
-        go(rc(blk, kvx_s.at[p, 0], kvx_r.at[p, 0], right))
-        go(rc(blk, kvx_s.at[p, 1], kvx_r.at[p, 1], left))
-        go(rc(blk, kvd_s.at[p, 0], kvd_r.at[p, 0], sib))
-
-    low, high = pl.ds(0, 96), pl.ds(96, KVR - 96)
-
-    def x_relay(p):
-        ref = kv.at[p, c, xl]
-        rc(ref, kvx_s.at[p, 0], kvx_r.at[p, 0], right).wait_recv()
-        go(rc(kv.at[p, c, xl, low], kvx_s.at[p, 2], kvx_r.at[p, 2], right))
-        go(rc(ref, kvd_s.at[p, 1], kvd_r.at[p, 1], sib))
-        ref = kv.at[p, c, xr]
-        rc(ref, kvx_s.at[p, 1], kvx_r.at[p, 1], left).wait_recv()
-        go(rc(kv.at[p, c, xr, high], kvx_s.at[p, 3], kvx_r.at[p, 3], left))
-        go(rc(ref, kvd_s.at[p, 2], kvd_r.at[p, 2], sib))
-
-    def x_end(p):
-        rc(kv.at[p, c, xo, low], kvx_s.at[p, 2], kvx_r.at[p, 2], right).wait_recv()
-        rc(kv.at[p, c, xo, high], kvx_s.at[p, 3], kvx_r.at[p, 3], left).wait_recv()
-        go(rc(kv.at[p, c, xo], kvd_s.at[p, 3], kvd_r.at[p, 3], sib))
-
-    def x_start_mixed(p, half):
-        rows = (low, high)[half]
-        for i, (to, dest) in enumerate(((right, xr), (left, xl), (across, xo))):
-            go_if((x < dest) if p == 0 else (x > dest),
-                  rc(kv.at[p, c, x, rows], kvm_s.at[p // 4, half, i], kvm_r.at[half, i], to))
-        if half == 1:
-            go_if(c == (0 if p == 0 else 1), rc(kv.at[p, c, x], kvd_s.at[p, 0], kvd_r.at[0, 0], sib))
-
-    def plane_of(p, xx):
-        return p if p > 0 else jnp.where(xx < x, 0, 4)
-
-    def x_end_mixed():
-        for i, xx in enumerate((xl, xr, xo)):
-            ref = kv.at[plane_of(0, xx), c, xx]
-            for half, rows in enumerate((low, high)):
-                rc(ref.at[rows], kvm_s.at[0, half, i], kvm_r.at[half, i], right).wait_recv()
-            go(rc(ref, kvd_s.at[0, i + 1], kvd_r.at[0, i + 1], sib))
-
-    def sib_wait(p):
-        own = p if p > 0 else jnp.where(c == 1, 0, 4)
-        for i, (pp, xx) in enumerate(((own, x), (plane_of(p, xl), xl), (plane_of(p, xr), xr), (plane_of(p, xo), xo))):
-            rc(kv.at[pp, oc, xx], kvd_s.at[p, i], kvd_r.at[p, i], sib).wait_recv()
-
-    def z_step(p):
-        for half in range(2):
-            z_copy(p - 1, half).wait_recv()
-            if p < DEPTH - 1:
-                go(z_copy(p, half))
-            else:
-                x_start_mixed(p, half)
-        if p < DEPTH - 1:
-            x_start(p)
-
-    def w_send(offset, i, dz):
-        go(rc(wz.at[lax.rem(z + offset, NZ), c], wz_s.at[i], wz_r.at[i], dev(dz=dz)))
-
-    def w_recv(i):
-        ref = wz.at[lax.rem(z + i, NZ), c]
-        rc(ref, wz_s.at[i], wz_r.at[i], up).wait_recv()
-        go(rc(ref, wd_s.at[i], wd_r.at[i], sib))
-
-    go(z_copy(0, 0))
+
     go(z_copy(0, 1))
-    x_start_mixed(0, 0)
     x_start_mixed(0, 1)
     loads[3].wait()
     w_send(0, 1, -1)
@@ -242,15 +244,19 @@
         early = [i * 2 + core < me for i in range(NX)]
         attend([(jnp.where(e, 0, 4), core, i) for i, e in enumerate(early)], [e | (z >= 4) for e in early], 480, after)
 
+    def a_copy(u, i):
+        return pltpu.make_async_remote_copy(
+            src_ref=ag.at[0, pl.ds(u * HALF, HALF)], dst_ref=ag.at[1 + u, pl.ds(i * HALF, HALF)],
+            send_sem=ax_s.at[u, i], recv_sem=ax_r.at[u, i], device_id=(right, left)[i], device_id_type=MESH)
+
     def a_send(u):
         mine = slice(u * HALF, (u + 1) * HALF)
         for h in range(HEADS):
             rows = slice((u * HEADS + h) * HALF, (u * HEADS + h + 1) * HALF)
             ag[0, mine, h * W:(h + 1) * W] = (acc[rows, 0:W] / acc[rows, W:2 * W]).astype(BF16)
-        for i, to in enumerate((right, left)):
-            go(pltpu.make_async_remote_copy(
-                src_ref=ag.at[0, pl.ds(u * HALF, HALF)], dst_ref=ag.at[1 + u, pl.ds(i * HALF, HALF)],
-                send_sem=ax_s.at[u, i], recv_sem=ax_r.at[u, i], device_id=to, device_id_type=MESH))
+        if u == 0:
+            a_copy(0, 0).start()
+            a_copy(0, 1).start()
 
     def a_far_copy(u, i):
         return pltpu.make_async_remote_copy(
@@ -289,8 +295,8 @@
     w_recv(2)
     w_send(2, 3, -1)
     w_send(2, 4, -2)
+    z_step(4)
     attend_plane(1)
-    z_step(4)
     x_end(2)
     x_relay(3)
     attend_plane(2)
@@ -374,6 +380,9 @@
         return slot == 3 or (slot != 1 and half == 1)
 
     send_step(0, 0)
+    for i in range(2):
+        a_copy(0, i).wait_send()
+        go(a_copy(1, i))
     a_near(0)
     send_step(0, 1)
 
@@ -406,12 +415,9 @@
     send_step(3, 2)
     send_step(3, 0)
     finish(1)
+    finish(3)
     finish(2)
-    finish(3)
     finish(0)
-    for j in (1, 2, 3):
-        for i in range(2):
-            fx(j, i).wait_recv()
 
     def main_of(i, u):
         return fin[i, u, GROUP:GROUP + HALF, :] if second(i, u) else fin[i, u, 0:HALF, :]
@@ -419,13 +425,25 @@
     def rest_of(i, u):
         return fin[i, u, 0:GROUP, :] if second(i, u) else fin[i, u, HALF:HALF + GROUP, :]
 
-    for u in range(2):
-        main = jnp.dot(jnp.concatenate([main_of(i, u) for i in range(NX)], axis=1), selm[...], preferred_element_type=F32)
-        rest = jnp.concatenate([rest_of(i, u) for i in range(NX)], axis=1)
-        for g in range(2):
-            add = jnp.dot(rest, selr[2 * u + g], preferred_element_type=F32)
-            o_ref[u * HALF + g * GROUP:u * HALF + (g + 1) * GROUP, :] = (
-                main[g * GROUP:(g + 1) * GROUP] + add).astype(BF16)
+    def place(slots):
+        lanes = slice(slots[0] * W, (slots[-1] + 1) * W)
+        halves = []
+        for u in range(2):
+            main = jnp.dot(jnp.concatenate([main_of(i, u) for i in slots], axis=1), selm[lanes, :], preferred_element_type=F32)
+            rest = jnp.concatenate([rest_of(i, u) for i in slots], axis=1)
+            add = [jnp.dot(rest, selr[2 * u + g, lanes, :], preferred_element_type=F32) for g in range(2)]
+            halves.append(main + jnp.concatenate(add, axis=0))
+        return jnp.concatenate(halves, axis=0)
+
+    for i in range(2):
+        fx(3, i).wait_recv()
+    out[...] = place((2,))
+    fx(1, 0).wait_recv()
+    fx(2, 0).wait_recv()
+    out[...] += place((0, 1))
+    fx(1, 1).wait_recv()
+    fx(2, 1).wait_recv()
+    o_ref[...] = (out[...] + place((3,))).astype(BF16)
 
     for copy, cond in started:
         if cond is None:
@@ -459,6 +477,7 @@
             pltpu.VMEM((NX, 2, HALF + GROUP, W), BF16),
             pltpu.VMEM((NX * W, K), BF16),
             pltpu.VMEM((4, NX * W, K), BF16),
+            pltpu.VMEM((T, K), F32),
             sem((5,)), sem((4, 2)), sem((4, 2)), sem((4, 4)), sem((4, 4)), sem((2, 2, 3)), sem((2, 3)), sem((5, 4)), sem((5, 4)),
             sem((8,)), sem((8,)), sem((8,)), sem((8,)),
             sem((2, 4)), sem((2, 4)), sem((2, 4, NX)), sem((2, 4, NX)), sem((6,)), sem((6,)),

time: 81.9 us -> 78.5 us (0.958)
  the two profiles are of different devices: /device:TPU:6 before, /device:TPU:16 now
where the time goes in v4:
time: 78.5 us; the launch traced here: 78.4 us
  Pallas kernels  77.7 us (99%)
    pallas_call x1, Pallas kernels, local(): pl.pallas_call(kernel, out_shape=pltpu.VMEM((T, K), BF16), in_specs=[pl.B...  77.7 us

profile of v4, /device:TPU:16, one launch (start us, length us, event | category | flops | bytes accessed | tf_op | source)
XLA Modules:
  0.0 78.4 jit_solution(9950102571945420523)
XLA Ops:
  0.0 77.7 %attend_project.1 = bf16[192,640]{1,0:T(8,128)(2,1)S(1)} custom-call(bf16[192,640]{1,0:T(8,128)(2,1)} %q_hbm.1, bf16[192,128]{1,0:T(8,128)(2,1)} %k_hbm.1, bf16[192,128]{1,0:T(8,128)(2,1)} %v_hbm.1, s32[1,192]{1,0:T(1,128)} %bitcast.3, bf16[80,640]{1,0:T(8,128)(2,1)} %bitcast.2), custom_call_target="tpu_custom_call" | custom-call | tf_op jit(solution)/shard_map/attend_project/pallas_call | solution.py:458
  77.7 0.7 copy.7

commit v5 on v4

--- a/solution.py
+++ b/solution.py
@@ -57,7 +57,7 @@
             src_ref=ref, dst_ref=ref, send_sem=ss, recv_sem=rs, device_id=to, device_id_type=MESH)
 
     barrier = pltpu.get_barrier_semaphore()
-    peers = [dev(dz=i) for i in (1, -1, 2, -2)] + [right, left, across, sib] + [dev(dy=i) for i in (1, -1, 2, -2)]
+    peers = [dev(dz=i) for i in (1, -1, 2, -2)] + [right, left, across, sib] + [dev(dy=i) for i in (1, -1)]
     for peer in peers:
         pl.semaphore_signal(barrier, inc=1, device_id=peer, device_id_type=MESH)
     loads = [
@@ -328,11 +328,10 @@
         return 4 if (d + j) % 2 == 1 else 3
 
     def rs(d, r, j):
-        leap = 2 if (j == 3 and r == 4) else 1
         return pltpu.make_async_remote_copy(
             src_ref=sbuf.at[d, r - 1, j], dst_ref=rbuf.at[d, r - 1, j],
             send_sem=rs_s.at[d, r - 1, j], recv_sem=rs_r.at[d, r - 1, j],
-            device_id=dev(dy=leap if d == 0 else -leap), device_id_type=MESH)
+            device_id=dev(dy=1 if d == 0 else -1), device_id_type=MESH)
 
     def send_block(d, r, j, arrived):
         total = partial(j, lax.rem(t + r, NY) if d == 0 else lax.rem(t - r + NY, NY))
@@ -344,14 +343,8 @@
 
     def send_step(n, j):
         for d in range(2):
-            if j == 3 and hops(d, j) == 4:
-                if n == 0:
-                    send_block(d, 4, j, ())
-                r = 3 - n
-                arrived = () if n == 0 else (4, 3) if n == 1 else (2,)
-            else:
-                r = hops(d, j) - n
-                arrived = () if n == 0 else (r + 1,)
+            r = hops(d, j) - n
+            arrived = () if n == 0 else (r + 1,)
             if r > 0:
                 send_block(d, r, j, arrived)
 
@@ -413,6 +406,7 @@
     send_step(3, 1)
     send_step(2, 3)
     send_step(3, 2)
+    send_step(3, 3)
     send_step(3, 0)
     finish(1)
     finish(3)

time: 78.5 us -> 77.6 us (0.989)
  the two profiles are of different devices: /device:TPU:16 before, /device:TPU:6 now
where the time goes in v5:
time: 77.6 us; the launch traced here: 76.9 us
  Pallas kernels  76.2 us (98%)
    pallas_call x1, Pallas kernels, local(): pl.pallas_call(kernel, out_shape=pltpu.VMEM((T, K), BF16), in_specs=[pl.B...  76.2 us

profile of v5, /device:TPU:6, one launch (start us, length us, event | category | flops | bytes accessed | tf_op | source)
XLA Modules:
  0.0 76.9 jit_solution(1595652449271857252)
XLA Ops:
  0.0 76.2 %attend_project.1 = bf16[192,640]{1,0:T(8,128)(2,1)S(1)} custom-call(bf16[192,640]{1,0:T(8,128)(2,1)} %q_hbm.1, bf16[192,128]{1,0:T(8,128)(2,1)} %k_hbm.1, bf16[192,128]{1,0:T(8,128)(2,1)} %v_hbm.1, s32[1,192]{1,0:T(1,128)} %bitcast.3, bf16[80,640]{1,0:T(8,128)(2,1)} %bitcast.2), custom_call_target="tpu_custom_call" | custom-call | tf_op jit(solution)/shard_map/attend_project/pallas_call | solution.py:452
  76.2 0.7 copy.7
